TPU v7x, 512 devices: a whole 4x8x8 slice. The times are simulated.
512 devices in a mesh: row: 32 (over x, y), col: 16 (over z, core).
Axes of the slice: x: 4, y: 8, z: 8, core: 2. Of those that a mesh axis runs over, the one named last changes fastest.
Arguments:
- activations: bfloat16 [512, 8192], P('row', 'col'), may hold values from -6 to 6
- out_grad: bfloat16 [512, 8192], P('row', 'col'), may hold values from -1.5 to 1.5
- w_gate: bfloat16 [8192, 14336], P('col', 'row'), may hold values from -0.0625 to 0.0625
- w_up: bfloat16 [8192, 14336], P('col', 'row'), may hold values from -0.0625 to 0.0625
- w_down: bfloat16 [14336, 8192], P('row', 'col'), may hold values from -0.046875 to 0.046875
Outputs:
- in_grad: bfloat16 [512, 8192], P('row', 'col')
- grad_gate: bfloat16 [8192, 14336], P('col', 'row')
- grad_up: bfloat16 [8192, 14336], P('col', 'row')
- grad_down: bfloat16 [14336, 8192], P('row', 'col')
All inputs are finite; a program needn't handle non-finite values.
Results may differ from a plain program's by a relative error of at most 0.0049.
Values may be sent and summed in bfloat16 or wider, within the bound.
No kernel may reach another device: no remote copies, remote signals or barrier semaphores. Data moves between devices by JAX's collectives and lax.ppermute only.
A program may use at most 64 MiB of HBM per device.

v0:
```python
import jax
import jax.numpy as jnp
from jax import lax
from jax.sharding import PartitionSpec as P


def swiglu_parts(summed, width):
    gate = summed[:, :width]
    up_val = summed[:, width : 2 * width]
    hidden_grad = summed[:, 2 * width :]
    sigma = jax.nn.sigmoid(gate)
    hidden = (gate * sigma * up_val).astype(jnp.bfloat16)
    up_grad = (hidden_grad * gate * sigma).astype(jnp.bfloat16)
    gate_grad = (hidden_grad * up_val * sigma * (1.0 + gate * (1.0 - sigma))).astype(jnp.bfloat16)
    return (hidden, gate_grad, up_grad)


def on_device(activations, out_grad, w_gate, w_up, w_down):
    inputs, grads = (
        lax.all_gather(activations, "row", axis=0, tiled=True),
        lax.all_gather(out_grad, "row", axis=0, tiled=True),
    )
    width = w_gate.shape[1]
    contract_last = (((1,), (1,)), ((), ()))
    contract_first = (((0,), (0,)), ((), ()))
    gate_part = jnp.dot(inputs, w_gate, preferred_element_type=jnp.float32)
    up_part = jnp.dot(inputs, w_up, preferred_element_type=jnp.float32)
    back_part = lax.dot_general(grads, w_down, contract_last, preferred_element_type=jnp.float32)
    summed = lax.psum(jnp.concatenate([gate_part, up_part, back_part], axis=1), "col")
    hidden, gate_grad, up_grad = swiglu_parts(summed, width)
    grad_down = lax.dot_general(
        hidden, grads, contract_first, preferred_element_type=jnp.float32
    ).astype(jnp.bfloat16)
    grad_gate = lax.dot_general(
        inputs, gate_grad, contract_first, preferred_element_type=jnp.float32
    ).astype(jnp.bfloat16)
    grad_up = lax.dot_general(
        inputs, up_grad, contract_first, preferred_element_type=jnp.float32
    ).astype(jnp.bfloat16)
    term = lax.dot_general(gate_grad, w_gate, contract_last, preferred_element_type=jnp.float32)
    in_grad = lax.psum_scatter(
        term + lax.dot_general(up_grad, w_up, contract_last, preferred_element_type=jnp.float32),
        "row",
        scatter_dimension=0,
        tiled=True,
    ).astype(jnp.bfloat16)
    return (in_grad, grad_gate, grad_up, grad_down)


def solution(mesh):
    placed = (P("row", "col"), P("row", "col"), P("col", "row"), P("col", "row"), P("row", "col"))
    return jax.shard_map(
        on_device,
        mesh=mesh,
        in_specs=placed,
        out_specs=(P("row", "col"), P("col", "row"), P("col", "row"), P("row", "col")),
        check_vma=False,
    )
```

profile of v0, /device:TPU:1, one launch (start us, length us, event | category | flops | bytes accessed | tf_op | source)
XLA Modules:
  0.0 463.0 jit_solution(9016981276234291277)
XLA Ops:
  7.2 0.0 copy-start
  7.2 0.0 copy-start.2
  7.2 0.0 all-reduce.2.cloned.1.call-start
  7.2 40.0 %all_gather.6 = bf16[512,512]{1,0:T(8,128)(2,1)S(1)} all-gather(bf16[16,512]{1,0:T(8,128)(2,1)} %param.5), channel_id=1, replica_groups=mesh['row'=32,'col'=16] {'row'}, dimensions={0}, use_global_device_ids=true | all-gather | bytes 540672 | tf_op jit(solution)/shard_map/all_gather | solution.py:20
  47.2 35.9 %all_gather.7 = bf16[512,512]{1,0:T(8,128)(2,1)S(1)} all-gather(bf16[16,512]{1,0:T(8,128)(2,1)} %param.6), channel_id=1, replica_groups=mesh['row'=32,'col'=16] {'row'}, dimensions={0}, use_global_device_ids=true | all-gather | bytes 540672 | tf_op jit(solution)/shard_map/all_gather | solution.py:21
  83.1 1.4 fusion.4
  84.6 0.0 copy-done
  84.6 0.4 fusion.3
  85.0 0.0 copy-done.2
  85.0 0.4 fusion.5
  85.5 1.8 pad_maximum_fusion
  87.3 0.0 all-reduce.2.cloned.1.call-update
  87.3 0.0 copy-start.1
  87.3 0.0 reduce-scatter.2.cloned.1.call-start
  87.4 148.2 %all-reduce.2.cloned.1.call-done = f32[512,1344]{0,1:T(8,128)} async-done(((f32[512,1344]{0,1:T(8,128)}), f32[512,1344]{0,1:T(8,128)}) %all-reduce.2.cloned.1.call-update) | async-done | bytes 2752528 | tf_op jit(solution)/shard_map/psum | solution.py:29
  235.6 2.2 multiply_convert_fusion.1
  237.8 0.5 fusion.6
  238.3 0.0 copy-done.1
  238.3 1.5 convolution_add_fusion
  239.7 0.0 reduce-scatter.2.cloned.1.call-update
  239.8 1.2 fusion.1
  240.9 1.2 fusion
  242.1 2.6 convolution_convert_fusion
  244.8 210.1 %reduce-scatter.2.cloned.1.call-done = f32[16,512]{1,0:T(8,128)} async-done(((f32[512,512]{1,0:T(8,128)}), f32[16,512]{1,0:T(8,128)}) %reduce-scatter.2.cloned.1.call-update) | async-done | bytes 32784 | tf_op jit(solution)/shard_map/reduce_scatter | solution.py:41
  454.8 1.4 convert_element_type.29
Async XLA Ops:
  7.2 77.4 %copy-start = (bf16[512,448]{0,1:T(8,128)(2,1)S(1)}, bf16[512,448]{0,1:T(8,128)(2,1)}, u32[]{:S(2)}) copy-start(bf16[512,448]{0,1:T(8,128)(2,1)} %param.7) | copy-start | bytes 1376260
  7.2 77.8 %copy-start.2 = (bf16[448,512]{1,0:T(8,128)(2,1)S(1)}, bf16[448,512]{1,0:T(8,128)(2,1)}, u32[]{:S(2)}) copy-start(bf16[448,512]{1,0:T(8,128)(2,1)} %param.9) | copy-start | bytes 1376260
  7.2 228.4 %all-reduce.2.cloned.1.call-start = ((), (), s32[]{:S(2)}) async-start(), calls=%async_computation.1 | async-start | bytes 5505024 | tf_op jit(solution)/shard_map/psum | solution.py:29
  87.3 151.0 %copy-start.1 = (bf16[512,448]{0,1:T(8,128)(2,1)S(1)}, bf16[512,448]{0,1:T(8,128)(2,1)}, u32[]{:S(2)}) copy-start(bf16[512,448]{0,1:T(8,128)(2,1)} %param.8) | copy-start | bytes 1376260
  87.3 367.5 %reduce-scatter.2.cloned.1.call-start = ((), (), s32[]{:S(2)}) async-start(), calls=%async_computation.2 | async-start | bytes 1081344 | tf_op jit(solution)/shard_map/reduce_scatter | solution.py:41
Sparse Core Ops, SparseCore 0:
  87.4 148.0 all-reduce.1
  240.6 214.1 reduce-scatter.1
where the time goes:
time: 468 us; the launch traced here: 463 us
  waiting for transfers between devices  358 us (76%)
  blocking collectives  75.9 us (16%)
  between operations  14.1 us (3%)
  matrix products  9.21 us (2%)
  other arithmetic  5.44 us (1%)
    reduce_scatter x1, waiting for transfers between devices, on_device(): lax.psum_scatter(term + lax.dot_general(up_grad, w_up, contract_last, pre...  210 us
    psum x1, waiting for transfers between devices, on_device(): lax.psum(jnp.concatenate([gate_part, up_part, back_part], axis=1), 'col')  148 us
    all_gather x1, blocking collectives, on_device(): lax.all_gather(activations, 'row', axis=0, tiled=True)  40 us
    all_gather x1, blocking collectives, on_device(): lax.all_gather(out_grad, 'row', axis=0, tiled=True)  35.9 us
  transfers between devices with their start and end apart: 2, of which 2 were waited for; matrix products, arithmetic and copies ran while one was open for 1% of the time, Pallas kernels for 0%

commit v1 on v0

v1 whole, which is shorter than its diff:
```python
import jax
import jax.numpy as jnp
from jax import lax
from jax.sharding import Mesh
from jax.sharding import PartitionSpec as P

X, Y, Z = 4, 8, 8
ROW = ("x", "y")
COL = ("z", "core")
SWAP = ((0, 1), (1, 0))


def gather(block, axis, count):
    return lax.all_to_all(jnp.broadcast_to(block[None], (count,) + block.shape), axis, 0, 0)


def swiglu_parts(gate, up_val, hidden_grad):
    sigma = jax.nn.sigmoid(gate)
    hidden = (gate * sigma * up_val).astype(jnp.bfloat16)
    up_grad = (hidden_grad * gate * sigma).astype(jnp.bfloat16)
    gate_grad = (hidden_grad * up_val * sigma * (1.0 + gate * (1.0 - sigma))).astype(jnp.bfloat16)
    return jnp.stack([hidden, gate_grad, up_grad])


def product(a, b, contract_a, contract_b):
    return lax.dot_general(
        a, b, (((contract_a,), (contract_b,)), ((), ())), preferred_element_type=jnp.float32
    )


def on_device(activations, out_grad, w_gate, w_up, w_down):
    tokens, width = activations.shape
    units = w_gate.shape[1]
    first = lax.axis_index("core") == 0
    both = gather(jnp.concatenate([activations, out_grad], axis=1), "y", Y)
    both = gather(both.reshape(Y * tokens, 2 * width), "x", X).reshape(X * Y * tokens, 2 * width)
    inputs, grads = both[:, :width], both[:, width:]
    half = inputs.shape[0] // 2

    parts = jnp.stack(
        [product(w_gate, inputs, 0, 1), product(w_up, inputs, 0, 1), product(w_down, grads, 1, 1)]
    )
    low, high = parts[..., :half], parts[..., half:]
    other = lax.ppermute(jnp.where(first, high, low), "core", SWAP)
    chip = (jnp.where(first, low, high) + other).astype(jnp.bfloat16)
    rows = units // Z
    sent = chip.reshape(3, Z, rows, half).transpose(1, 0, 2, 3)
    summed = jnp.sum(lax.all_to_all(sent, "z", 0, 0).astype(jnp.float32), axis=0)

    mine = swiglu_parts(summed[0], summed[1], summed[2])
    own = gather(mine, "z", Z)
    other = lax.ppermute(own, "core", SWAP)
    whole = jnp.where(
        first, jnp.concatenate([own, other], axis=3), jnp.concatenate([other, own], axis=3)
    )
    hidden, gate_grad, up_grad = whole.transpose(1, 0, 2, 3).reshape(3, units, 2 * half)

    term = product(gate_grad, w_gate, 0, 1) + product(up_grad, w_up, 0, 1)
    terms = lax.all_to_all(term.reshape(X * Y, tokens, width), ROW, 0, 0)
    in_grad = jnp.sum(terms, axis=0).astype(jnp.bfloat16)
    grad_down = product(hidden, grads, 1, 0).astype(jnp.bfloat16)
    grad_gate = product(inputs, gate_grad, 0, 1).astype(jnp.bfloat16)
    grad_up = product(inputs, up_grad, 0, 1).astype(jnp.bfloat16)
    return (in_grad, grad_gate, grad_up, grad_down)


def solution(mesh):
    grid = Mesh(mesh.devices.reshape(X, Y, Z, 2), ROW + COL)
    return jax.shard_map(
        on_device,
        mesh=grid,
        in_specs=(P(ROW, COL), P(ROW, COL), P(COL, ROW), P(COL, ROW), P(ROW, COL)),
        out_specs=(P(ROW, COL), P(COL, ROW), P(COL, ROW), P(ROW, COL)),
        check_vma=False,
    )
```

time: 468 us -> 142 us (0.30)
  the two profiles are of different devices: /device:TPU:1 before, /device:TPU:8 now
where the time goes in v1:
time: 142 us
  blocking collectives  71.8 us (51%)
  waiting for transfers between devices  42.9 us (30%)
  starting transfers between devices  14.2 us (10%)
  matrix products  6.75 us (5%)
  other arithmetic  2.76 us (2%)
  local copies, waits for them, and re-layouts  2.69 us (2%)
    all_to_all x2, blocking collectives, gather(): lax.all_to_all(jnp.broadcast_to(block[None], (count,) + block.shape), axi...  40.4 us
    all_to_all x1, blocking collectives, on_device(): lax.all_to_all(sent, 'z', 0, 0).astype(jnp.float32)  31.4 us
    all_to_all x1, waiting for transfers between devices, on_device(): terms = lax.all_to_all(term.reshape(X * Y, tokens, width), ROW, 0, 0)  25.2 us
    all_to_all x1, waiting for transfers between devices, gather(): lax.all_to_all(jnp.broadcast_to(block[None], (count,) + block.shape), axi...  12.5 us
    dot_general x8, matrix products, product(): lax.dot_general(a, b, (((contract_a,), (contract_b,)), ((), ())), preferr...  6.75 us
    all_to_all x1, starting transfers between devices, on_device(): terms = lax.all_to_all(term.reshape(X * Y, tokens, width), ROW, 0, 0)  6.05 us
    all_to_all x1, starting transfers between devices, gather(): lax.all_to_all(jnp.broadcast_to(block[None], (count,) + block.shape), axi...  4.29 us
    ppermute x1, waiting for transfers between devices, on_device(): other = lax.ppermute(jnp.where(first, high, low), 'core', SWAP)  3.09 us
  transfers between devices with their start and end apart: 4, of which 4 were waited for; matrix products, arithmetic and copies ran while one was open for 2% of the time, Pallas kernels for 0%

profile of v1, /device:TPU:8, one launch (start us, length us, event | category | flops | bytes accessed | tf_op | source)
XLA Modules:
  0.0 141.8 jit_solution(9277846583589267941)
XLA Ops:
  0.6 0.0 copy-start
  0.6 0.8 pad_maximum_fusion.2
  1.5 17.8 %all_to_all.25 = bf16[8,16,1024]{2,1,0:T(8,128)(2,1)S(1)} all-to-all(bf16[8,16,1024]{2,1,0:T(8,128)(2,1)S(1)} %broadcast_in_dim.8), channel_id=1, replica_groups=mesh['x'=4,'y'=8,'z'=8,'core'=2] {'y'}, dimensions={0} | all-to-all | bytes 524288 | tf_op jit(solution)/shard_map/all_to_all | solution.py:14
  19.2 1.1 broadcast_in_dim.10
  20.3 4.3 %all-to-all-start.1 = ((bf16[4,128,1024]{2,1,0:T(8,128)(2,1)}), bf16[4,128,1024]{2,1,0:T(8,128)(2,1)S(1)}, u32[]{:S(2)}, u32[]{:S(2)}) async-start(bf16[4,128,1024]{2,1,0:T(8,128)(2,1)} %broadcast_in_dim.10), calls=%async_computation.1 | async-start | bytes 2097152 | tf_op jit(solution)/shard_map/all_to_all | solution.py:14
  24.6 12.5 %all-to-all-done.1 = bf16[4,128,1024]{2,1,0:T(8,128)(2,1)S(1)} async-done(((bf16[4,128,1024]{2,1,0:T(8,128)(2,1)}), bf16[4,128,1024]{2,1,0:T(8,128)(2,1)S(1)}, u32[]{:S(2)}, u32[]{:S(2)}) %all-to-all-start.1) | async-done | bytes 1048608 | tf_op jit(solution)/shard_map/all_to_all | solution.py:14
  37.1 0.4 convolution_bitcast_fusion.1
  37.6 0.0 copy-start.1
  37.6 0.4 convolution_bitcast_fusion
  38.0 0.6 copy-done.1
  38.6 0.4 convolution_bitcast_fusion.2
  39.1 0.3 pad_maximum_fusion
  39.3 0.2 slice_select_fusion
  39.5 1.9 %collective-permute-start = (f32[3,448,256]{2,1,0:T(8,128)S(1)}, f32[3,448,256]{2,1,0:T(8,128)S(1)}, u32[]{:S(2)}, u32[]{:S(2)}) collective-permute-start(f32[3,448,256]{2,1,0:T(8,128)S(1)} %slice_select_fusion), channel_id=1, source_target_pairs={{0,1},{1,0},{2,3},{3,2},{4,5},{5,4},{6,7},{7,6},{8,9},{9,8},{10,11... | collective-permute-start | bytes 4128776 | tf_op jit(solution)/shard_map/ppermute | solution.py:44
  41.4 3.1 %collective-permute-done = f32[3,448,256]{2,1,0:T(8,128)S(1)} collective-permute-done((f32[3,448,256]{2,1,0:T(8,128)S(1)}, f32[3,448,256]{2,1,0:T(8,128)S(1)}, u32[]{:S(2)}, u32[]{:S(2)}) %collective-permute-start) | collective-permute-done | bytes 1376288 | tf_op jit(solution)/shard_map/ppermute | solution.py:44
  44.5 0.3 add_convert_fusion
  44.9 31.4 %all_to_all.26 = bf16[8,3,56,256]{3,2,1,0:T(8,128)(2,1)S(1)} all-to-all(bf16[8,3,56,256]{3,2,1,0:T(8,128)(2,1)S(1)} %bitcast.41), channel_id=1, replica_groups=mesh['x'=4,'y'=8,'z'=8,'core'=2] {'z'}, dimensions={0} | all-to-all | bytes 1376256 | tf_op jit(solution)/shard_map/all_to_all | solution.py:48
  76.3 0.1 convert_reduce_fusion
  76.5 22.6 %all_to_all.27 = bf16[8,3,56,256]{3,2,1,0:T(8,128)(2,1)S(1)} all-to-all(bf16[8,3,56,256]{3,2,1,0:T(8,128)(2,1)S(1)} %broadcast_in_dim.22), channel_id=1, replica_groups=mesh['x'=4,'y'=8,'z'=8,'core'=2] {'z'}, dimensions={0} | all-to-all | bytes 1376256 | tf_op jit(solution)/shard_map/all_to_all | solution.py:14
  99.2 1.9 %collective-permute-start.1 = (bf16[8,3,56,256]{3,2,1,0:T(8,128)(2,1)S(1)}, bf16[8,3,56,256]{3,2,1,0:T(8,128)(2,1)S(1)}, u32[]{:S(2)}, u32[]{:S(2)}) collective-permute-start(bf16[8,3,56,256]{3,2,1,0:T(8,128)(2,1)S(1)} %all_to_all.27), channel_id=1, source_target_pairs={{0,1},{1,0},{2,3},{3,2},{4,5},{5,4},{6,7},{7,6},{8,9},{9,8},{10,11... | collective-permute-start | bytes 2064392 | tf_op jit(solution)/shard_map/ppermute | solution.py:52
  101.1 2.1 %collective-permute-done.1 = bf16[8,3,56,256]{3,2,1,0:T(8,128)(2,1)S(1)} collective-permute-done((bf16[8,3,56,256]{3,2,1,0:T(8,128)(2,1)S(1)}, bf16[8,3,56,256]{3,2,1,0:T(8,128)(2,1)S(1)}, u32[]{:S(2)}, u32[]{:S(2)}) %collective-permute-start.1) | collective-permute-done | bytes 688160 | tf_op jit(solution)/shard_map/ppermute | solution.py:52
  103.2 0.4 fusion
  103.6 0.9 fusion.7
  104.5 0.5 fusion.8
  104.9 1.4 %convolution_add_fusion = f32[512,512]{1,0:T(8,128)} fusion(f32[512,512]{1,0:T(8,128)S(1)} %fusion.8, bf16[448,512]{1,0:T(8,128)(2,1)S(1)} %bitcast.42, bf16[512,448]{0,1:T(8,128)(2,1)S(1)} %copy-done.1), kind=kOutput, calls=%fused_computation.5 | convolution fusion | flops 235143168 | bytes 3014656 | tf_op jit(solution)/shard_map/dot_general | solution.py:26
  106.4 6.1 %all-to-all-start.4 = ((f32[32,16,512]{2,1,0:T(8,128)}), f32[32,16,512]{2,1,0:T(8,128)S(1)}, u32[]{:S(2)}, u32[]{:S(2)}) async-start(f32[32,16,512]{2,1,0:T(8,128)} %bitcast.13), calls=%async_computation.4 | async-start | bytes 2097152 | tf_op jit(solution)/shard_map/all_to_all | solution.py:59
  112.4 0.0 copy-start.3
  112.4 1.2 convolution_convert_fusion
  113.6 1.2 convolution_convert_fusion.1
  114.8 1.2 convolution_convert_fusion.2
  116.0 25.2 %all-to-all-done.4 = f32[32,16,512]{2,1,0:T(8,128)S(1)} async-done(((f32[32,16,512]{2,1,0:T(8,128)}), f32[32,16,512]{2,1,0:T(8,128)S(1)}, u32[]{:S(2)}, u32[]{:S(2)}) %all-to-all-start.4) | async-done | bytes 1048608 | tf_op jit(solution)/shard_map/all_to_all | solution.py:59
  141.2 0.7 reduce_sum.19
  (9 shorter events, 0.2 us)
Async XLA Ops:
  0.6 36.5 %copy-start = (bf16[512,448]{0,1:T(8,128)(2,1)S(1)}, bf16[512,448]{0,1:T(8,128)(2,1)}, u32[]{:S(2)}) copy-start(bf16[512,448]{0,1:T(8,128)(2,1)} %param.8) | copy-start | bytes 1376260
  20.3 16.8 %all-to-all-start.1 = ((bf16[4,128,1024]{2,1,0:T(8,128)(2,1)}), bf16[4,128,1024]{2,1,0:T(8,128)(2,1)S(1)}, u32[]{:S(2)}, u32[]{:S(2)}) async-start(bf16[4,128,1024]{2,1,0:T(8,128)(2,1)} %broadcast_in_dim.10), calls=%async_computation.1 | async-start | bytes 2097152 | tf_op jit(solution)/shard_map/all_to_all | solution.py:14
  24.6 13.0 %copy-start.2 = (bf16[448,512]{1,0:T(8,128)(2,1)S(1)}, bf16[448,512]{1,0:T(8,128)(2,1)}, u32[]{:S(2)}) copy-start(bf16[448,512]{1,0:T(8,128)(2,1)} %param.9) | copy-start | bytes 1376260
  37.6 1.0 copy-start.1
  39.5 5.0 %collective-permute-start = (f32[3,448,256]{2,1,0:T(8,128)S(1)}, f32[3,448,256]{2,1,0:T(8,128)S(1)}, u32[]{:S(2)}, u32[]{:S(2)}) collective-permute-start(f32[3,448,256]{2,1,0:T(8,128)S(1)} %slice_select_fusion), channel_id=1, source_target_pairs={{0,1},{1,0},{2,3},{3,2},{4,5},{5,4},{6,7},{7,6},{8,9},{9,8},{10,11... | collective-permute-start | bytes 4128776 | tf_op jit(solution)/shard_map/ppermute | solution.py:44
  99.2 4.0 %collective-permute-start.1 = (bf16[8,3,56,256]{3,2,1,0:T(8,128)(2,1)S(1)}, bf16[8,3,56,256]{3,2,1,0:T(8,128)(2,1)S(1)}, u32[]{:S(2)}, u32[]{:S(2)}) collective-permute-start(bf16[8,3,56,256]{3,2,1,0:T(8,128)(2,1)S(1)} %all_to_all.27), channel_id=1, source_target_pairs={{0,1},{1,0},{2,3},{3,2},{4,5},{5,4},{6,7},{7,6},{8,9},{9,8},{10,11... | collective-permute-start | bytes 2064392 | tf_op jit(solution)/shard_map/ppermute | solution.py:52
  106.4 34.8 %all-to-all-start.4 = ((f32[32,16,512]{2,1,0:T(8,128)}), f32[32,16,512]{2,1,0:T(8,128)S(1)}, u32[]{:S(2)}, u32[]{:S(2)}) async-start(f32[32,16,512]{2,1,0:T(8,128)} %bitcast.13), calls=%async_computation.4 | async-start | bytes 2097152 | tf_op jit(solution)/shard_map/all_to_all | solution.py:59
  112.4 2.4 %copy-start.3 = (bf16[1,8,56,512]{3,2,0,1:T(8,128)(2,1)S(1)}, bf16[1,8,56,512]{3,2,0,1:T(8,128)(2,1)}, u32[]{:S(2)}) copy-start(bf16[1,8,56,512]{3,2,0,1:T(8,128)(2,1)} %get-tuple-element.4) | copy-start | bytes 1376260

commit v2 on v1

v2 whole, which is shorter than its diff:
```python
import jax
import jax.numpy as jnp
from jax import lax
from jax.experimental import pallas as pl
from jax.experimental.pallas import tpu as pltpu
from jax.sharding import Mesh
from jax.sharding import PartitionSpec as P

X, Y, Z = 4, 8, 8
ROW = ("x", "y")
COL = ("z", "core")
SWAP = ((0, 1), (1, 0))


def gather(block, axis, count):
    return lax.all_to_all(jnp.broadcast_to(block[None], (count,) + block.shape), axis, 0, 0)


def swiglu_parts(gate, up_val, hidden_grad):
    sigma = jax.nn.sigmoid(gate)
    hidden = (gate * sigma * up_val).astype(jnp.bfloat16)
    up_grad = (hidden_grad * gate * sigma).astype(jnp.bfloat16)
    gate_grad = (hidden_grad * up_val * sigma * (1.0 + gate * (1.0 - sigma))).astype(jnp.bfloat16)
    return jnp.stack([hidden, gate_grad, up_grad])


def product(a, b, contract_a, contract_b):
    out = lax.dot_general(
        a, b, (((contract_a,), (contract_b,)), ((), ())), preferred_element_type=jnp.float32
    )
    return out.astype(jnp.bfloat16)


def forward_kernel(mine_ref, other_ref, tokens_ref, out_ref):
    width = mine_ref.shape[2]
    total = lax.dot_general(
        mine_ref[0], tokens_ref[:, :width], (((1,), (1,)), ((), ())),
        preferred_element_type=jnp.float32,
    ) + lax.dot_general(
        other_ref[0], tokens_ref[:, width:], (((1,), (1,)), ((), ())),
        preferred_element_type=jnp.float32,
    )
    rows = out_ref.shape[2]
    for part in range(out_ref.shape[0]):
        out_ref[part, 0] = total[part * rows : (part + 1) * rows].astype(out_ref.dtype)


def forward(mine, other, tokens):
    _, units, width = mine.shape
    half = tokens.shape[0]
    block = pl.BlockSpec((1, units, width), lambda i: (i, 0, 0))
    return pl.pallas_call(
        forward_kernel,
        grid=(3,),
        in_specs=[block, block, pl.BlockSpec((half, 2 * width), lambda i: (0, i // 2))],
        out_specs=pl.BlockSpec((Z, 1, units // Z, half), lambda i: (0, i, 0, 0)),
        out_shape=jax.ShapeDtypeStruct((Z, 3, units // Z, half), jnp.bfloat16),
        compiler_params=pltpu.CompilerParams(vmem_limit_bytes=16 * 1024 * 1024),
        cost_estimate=pl.CostEstimate(
            flops=12 * units * width * half, bytes_accessed=16 * units * width, transcendentals=0
        ),
        name="forward",
    )(mine, other, tokens)


def on_device(activations, out_grad, w_gate, w_up, w_down):
    tokens, width = activations.shape
    units = w_gate.shape[1]
    few = tokens // 2
    half = X * Y * few
    first = lax.axis_index("core") == 0

    sent = jnp.concatenate([activations, out_grad], axis=1).reshape(1, 2, few, 2 * width)
    sent = jnp.broadcast_to(sent, (Y, 2, few, 2 * width)).reshape(2 * Y, few, 2 * width)
    got = lax.all_to_all(sent, ("y", "core"), 0, 0).reshape(Y, 2, few, 2, width)
    own = jnp.where(first, got[:, 0], got[:, 1])
    other = jnp.where(first, got[:, 1], got[:, 0])
    block = jnp.concatenate([own[:, :, 0], other[:, :, 0], own[:, :, 1], other[:, :, 1]], axis=2)
    both = gather(block.reshape(Y * few, 4 * width), "x", X).reshape(half, 4 * width)

    weights = jnp.stack([w_gate.T, w_up.T, w_down])
    swapped = lax.ppermute(weights, "core", SWAP)
    wide = jnp.concatenate([weights[:2], swapped[:2]], axis=2)
    rows = units // Z
    sent = forward(weights, swapped, both)
    summed = jnp.sum(lax.all_to_all(sent, "z", 0, 0).astype(jnp.float32), axis=0)
    mine = swiglu_parts(summed[0], summed[1], summed[2])
    own = gather(mine, "z", Z).transpose(1, 0, 2, 3).reshape(3, units, half)
    pair = own[1:]

    term = product(pair.reshape(2 * units, half), wide[:2].reshape(2 * units, 2 * width), 0, 0)
    terms = lax.all_to_all(term.reshape(X * Y, few, 2 * width), ROW, 0, 0)
    total = jnp.sum(terms.astype(jnp.float32), axis=0).astype(jnp.bfloat16)
    other = lax.ppermute(total[:, width:], "core", SWAP)
    in_grad = jnp.where(
        first,
        jnp.concatenate([total[:, :width], other]),
        jnp.concatenate([other, total[:, :width]]),
    )

    others = lax.ppermute(
        jnp.concatenate([both[:, width : 2 * width], both[:, 3 * width :]], axis=1), "core", SWAP
    )
    inputs = jnp.concatenate([both[:, :width], others[:, :width]])
    grads = jnp.concatenate([both[:, 2 * width : 3 * width], others[:, width:]])
    hidden, gate_grad, up_grad = jnp.concatenate(
        [own, lax.ppermute(own, "core", SWAP)], axis=2
    )

    grad_down = product(hidden, grads, 1, 0)
    grad_gate = product(inputs, gate_grad, 0, 1)
    grad_up = product(inputs, up_grad, 0, 1)
    return (in_grad, grad_gate, grad_up, grad_down)


def solution(mesh):
    grid = Mesh(mesh.devices.reshape(X, Y, Z, 2), ROW + COL)
    return jax.shard_map(
        on_device,
        mesh=grid,
        in_specs=(P(ROW, COL), P(ROW, COL), P(COL, ROW), P(COL, ROW), P(ROW, COL)),
        out_specs=(P(ROW, COL), P(COL, ROW), P(COL, ROW), P(ROW, COL)),
        check_vma=False,
    )
```

time: 142 us -> 127 us (0.89)
  the two profiles are of different devices: /device:TPU:8 before, /device:TPU:1 now
where the time goes in v2:
time: 127 us; the launch traced here: 126 us
  blocking collectives  46.8 us (37%)
  starting transfers between devices  33.7 us (27%)
  waiting for transfers between devices  28 us (22%)
  matrix products  5.04 us (4%)
  local copies, waits for them, and re-layouts  4.76 us (4%)
  other arithmetic  3.55 us (3%)
  Pallas kernels  2.99 us (2%)
    all_to_all x1, blocking collectives, on_device(): lax.all_to_all(sent, 'z', 0, 0).astype(jnp.float32)  28.8 us
    all_to_all x1, blocking collectives, gather(): lax.all_to_all(jnp.broadcast_to(block[None], (count,) + block.shape), axi...  18 us
    all_to_all x1, waiting for transfers between devices, gather(): lax.all_to_all(jnp.broadcast_to(block[None], (count,) + block.shape), axi...  16.6 us
    all_to_all x1, starting transfers between devices, on_device(): got = lax.all_to_all(sent, ('y', 'core'), 0, 0).reshape(Y, 2, few, 2, width)  10.2 us
    all_to_all x1, waiting for transfers between devices, on_device(): got = lax.all_to_all(sent, ('y', 'core'), 0, 0).reshape(Y, 2, few, 2, width)  8.26 us
    ppermute x1, starting transfers between devices, on_device(): other = lax.ppermute(total[:, width:], 'core', SWAP)  7.27 us
    dot_general x4, matrix products, product(): lax.dot_general(a, b, (((contract_a,), (contract_b,)), ((), ())), preferr...  5.04 us
    ppermute x1, starting transfers between devices, on_device(): lax.ppermute(jnp.concatenate([both[:, width:2 * width], both[:, 3 * width...  4.79 us
  transfers between devices with their start and end apart: 7, of which 4 were waited for; matrix products, arithmetic and copies ran while one was open for 7% of the time, Pallas kernels for 0%

profile of v2, /device:TPU:1, one launch (start us, length us, event | category | flops | bytes accessed | tf_op | source)
XLA Modules:
  0.0 125.8 jit_solution(10557555478947982656)
XLA Ops:
  0.6 0.7 maximum_bitcast_fusion.1
  1.4 0.7 broadcast_in_dim.21
  2.1 10.2 %all-to-all-start = ((bf16[16,8,1024]{2,1,0:T(8,128)(2,1)}), bf16[16,8,1024]{2,1,0:T(8,128)(2,1)S(1)}, u32[]{:S(2)}, u32[]{:S(2)}) async-start(bf16[16,8,1024]{2,1,0:T(8,128)(2,1)} %bitcast.6), calls=%async_computation | async-start | bytes 524288 | tf_op jit(solution)/shard_map/all_to_all | solution.py:75
  12.3 1.4 %pad_maximum_fusion.1.mine_ref = bf16[3,448,512]{2,1,0:T(8,128)(2,1)S(1)} fusion(bf16[1,448,512]{2,1,0:T(8,128)(2,1)} %bitcast.61, bf16[1,448,512]{2,1,0:T(8,128)(2,1)} %bitcast.56, bf16[1,448,512]{2,1,0:T(8,128)(2,1)} %bitcast.58), kind=kLoop, calls=%fused_computation.5 | loop fusion | flops 1376256 | bytes 2752512 | tf_op jit(solution)/shard_map/stack | solution.py:81
  13.7 2.1 %collective-permute-start = (bf16[3,448,512]{2,1,0:T(8,128)(2,1)S(1)}, bf16[3,448,512]{2,1,0:T(8,128)(2,1)}, u32[]{:S(2)}, u32[]{:S(2)}) collective-permute-start(bf16[3,448,512]{2,1,0:T(8,128)(2,1)S(1)} %pad_maximum_fusion.1.mine_ref), channel_id=1, source_target_pairs={{0,1},{1,0},{2,3},{3,2},{4,5},{5,4},{6,7},{7,6},{8,9},{9,8},{10,11... | collective-permute-start | bytes 4128776 | tf_op jit(solution)/shard_map/ppermute | solution.py:82
  15.9 8.3 %all-to-all-done = bf16[16,8,1024]{2,1,0:T(8,128)(2,1)S(1)} async-done(((bf16[16,8,1024]{2,1,0:T(8,128)(2,1)}), bf16[16,8,1024]{2,1,0:T(8,128)(2,1)S(1)}, u32[]{:S(2)}, u32[]{:S(2)}) %all-to-all-start) | async-done | bytes 262176 | tf_op jit(solution)/shard_map/all_to_all | solution.py:75
  24.2 0.2 reshape.47
  24.3 0.2 fusion.13
  24.6 0.5 fusion.21
  25.2 0.1 broadcast_in_dim.23
  25.3 18.0 %all_to_all.25 = bf16[4,64,2048]{2,1,0:T(8,128)(2,1)S(1)} all-to-all(bf16[4,64,2048]{2,1,0:T(8,128)(2,1)S(1)} %broadcast_in_dim.23), channel_id=1, replica_groups=mesh['x'=4,'y'=8,'z'=8,'core'=2] {'x'}, dimensions={0} | all-to-all | bytes 2097152 | tf_op jit(solution)/shard_map/all_to_all | solution.py:16
  43.3 3.0 %forward.1 = bf16[8,3,56,256]{3,2,1,0:T(8,128)(2,1)S(1)} custom-call(bf16[3,448,512]{2,1,0:T(8,128)(2,1)S(1)} %pad_maximum_fusion.1.mine_ref, bf16[3,448,512]{2,1,0:T(8,128)(2,1)} %collective-permute-done.other_ref, bf16[256,2048]{1,0:T(8,128)(2,1)S(1)} %bitcast.48), custom_call_target="tpu_custom_call" | custom-call | flops 704643072 | bytes 3670016 | tf_op jit(solution)/shard_map/forward/pallas_call | solution.py:52
  46.3 28.8 %all_to_all.26 = bf16[8,3,56,256]{3,2,1,0:T(8,128)(2,1)S(1)} all-to-all(bf16[8,3,56,256]{3,2,1,0:T(8,128)(2,1)S(1)} %forward.1), channel_id=1, replica_groups=mesh['x'=4,'y'=8,'z'=8,'core'=2] {'z'}, dimensions={0} | all-to-all | bytes 1376256 | tf_op jit(solution)/shard_map/all_to_all | solution.py:86
  75.1 0.1 convert_reduce_fusion
  75.3 0.9 broadcast_in_dim.24
  76.2 3.5 %all-to-all-start.3 = ((bf16[8,3,56,256]{3,2,1,0:T(8,128)(2,1)}), bf16[8,3,56,256]{3,2,1,0:T(8,128)(2,1)S(1)}, u32[]{:S(2)}, u32[]{:S(2)}) async-start(bf16[8,3,56,256]{3,2,1,0:T(8,128)(2,1)} %broadcast_in_dim.24), calls=%async_computation.3 | async-start | bytes 1376256 | tf_op jit(solution)/shard_map/all_to_all | solution.py:16
  79.8 0.9 fusion.18
  80.7 1.2 slice.92
  81.9 0.2 pad_maximum_fusion
  82.2 16.6 %all-to-all-done.3 = bf16[8,3,56,256]{3,2,1,0:T(8,128)(2,1)S(1)} async-done(((bf16[8,3,56,256]{3,2,1,0:T(8,128)(2,1)}), bf16[8,3,56,256]{3,2,1,0:T(8,128)(2,1)S(1)}, u32[]{:S(2)}, u32[]{:S(2)}) %all-to-all-start.3) | async-done | bytes 688160 | tf_op jit(solution)/shard_map/all_to_all | solution.py:16
  98.9 1.5 %fusion = bf16[32,8,1024]{2,1,0:T(8,128)(2,1)} fusion(bf16[896,256]{1,0:T(8,128)(2,1)S(1)} %bitcast.60, bf16[896,1024]{1,0:T(8,128)(2,1)S(1)} %bitcast.50), kind=kOutput, calls=%fused_computation.11 | convolution fusion | flops 470024192 | bytes 2818048 | tf_op jit(solution)/shard_map/dot_general | solution.py:28
  100.4 3.9 %all-to-all-start.4 = ((bf16[32,8,1024]{2,1,0:T(8,128)(2,1)}), bf16[32,8,1024]{2,1,0:T(8,128)(2,1)S(1)}, u32[]{:S(2)}, u32[]{:S(2)}) async-start(bf16[32,8,1024]{2,1,0:T(8,128)(2,1)} %fusion), calls=%async_computation.4 | async-start | bytes 1048576 | tf_op jit(solution)/shard_map/all_to_all | solution.py:92
  104.4 4.8 %collective-permute-start.2 = (bf16[256,1024]{1,0:T(8,128)(2,1)S(1)}, bf16[256,1024]{1,0:T(8,128)(2,1)S(1)}, u32[]{:S(2)}, u32[]{:S(2)}) collective-permute-start(bf16[256,1024]{1,0:T(8,128)(2,1)S(1)} %pad_maximum_fusion.2), channel_id=1, source_target_pairs={{0,1},{1,0},{2,3},{3,2},{4,5},{5,4},{6,7},{7,6},{8,9},{9,8},{10,11... | collective-permute-start | bytes 1572872 | tf_op jit(solution)/shard_map/ppermute | solution.py:101
  109.2 1.9 %collective-permute-start.3 = (bf16[3,448,256]{2,1,0:T(8,128)(2,1)S(1)}, bf16[3,448,256]{2,1,0:T(8,128)(2,1)S(1)}, u32[]{:S(2)}, u32[]{:S(2)}) collective-permute-start(bf16[3,448,256]{2,1,0:T(8,128)(2,1)S(1)} %bitcast.52), channel_id=1, source_target_pairs={{0,1},{1,0},{2,3},{3,2},{4,5},{5,4},{6,7},{7,6},{8,9},{9,8},{10,11... | collective-permute-start | bytes 2064392 | tf_op jit(solution)/shard_map/ppermute | solution.py:107
  111.2 2.1 %collective-permute-done.3 = bf16[3,448,256]{2,1,0:T(8,128)(2,1)S(1)} collective-permute-done((bf16[3,448,256]{2,1,0:T(8,128)(2,1)S(1)}, bf16[3,448,256]{2,1,0:T(8,128)(2,1)S(1)}, u32[]{:S(2)}, u32[]{:S(2)}) %collective-permute-start.3) | collective-permute-done | bytes 688160 | tf_op jit(solution)/shard_map/ppermute | solution.py:107
  113.2 1.2 convolution_convert_fusion.1
  114.4 1.2 convolution_convert_fusion.2
  115.6 1.0 all-to-all-done.4
  116.6 0.1 reduce_sum.22
  116.7 7.3 %collective-permute-start.1 = (bf16[8,512]{1,0:T(8,128)(2,1)S(1)}, bf16[8,512]{1,0:T(8,128)(2,1)S(1)}, u32[]{:S(2)}, u32[]{:S(2)}) collective-permute-start(bf16[8,512]{1,0:T(8,128)(2,1)S(1)} %get-tuple-element.22), channel_id=1, source_target_pairs={{0,1},{1,0},{2,3},{3,2},{4,5},{5,4},{6,7},{7,6},{8,9},{9,8},{10,11... | collective-permute-start | bytes 24584 | tf_op jit(solution)/shard_map/ppermute | solution.py:94
  124.0 1.2 convolution_convert_fusion.3
  125.1 0.6 maximum_select_fusion
  (25 shorter events, 0.3 us)
Async XLA Ops:
  2.1 22.1 %all-to-all-start = ((bf16[16,8,1024]{2,1,0:T(8,128)(2,1)}), bf16[16,8,1024]{2,1,0:T(8,128)(2,1)S(1)}, u32[]{:S(2)}, u32[]{:S(2)}) async-start(bf16[16,8,1024]{2,1,0:T(8,128)(2,1)} %bitcast.6), calls=%async_computation | async-start | bytes 524288 | tf_op jit(solution)/shard_map/all_to_all | solution.py:75
  13.7 29.6 %collective-permute-start = (bf16[3,448,512]{2,1,0:T(8,128)(2,1)S(1)}, bf16[3,448,512]{2,1,0:T(8,128)(2,1)}, u32[]{:S(2)}, u32[]{:S(2)}) collective-permute-start(bf16[3,448,512]{2,1,0:T(8,128)(2,1)S(1)} %pad_maximum_fusion.1.mine_ref), channel_id=1, source_target_pairs={{0,1},{1,0},{2,3},{3,2},{4,5},{5,4},{6,7},{7,6},{8,9},{9,8},{10,11... | collective-permute-start | bytes 4128776 | tf_op jit(solution)/shard_map/ppermute | solution.py:82
  76.2 22.6 %all-to-all-start.3 = ((bf16[8,3,56,256]{3,2,1,0:T(8,128)(2,1)}), bf16[8,3,56,256]{3,2,1,0:T(8,128)(2,1)S(1)}, u32[]{:S(2)}, u32[]{:S(2)}) async-start(bf16[8,3,56,256]{3,2,1,0:T(8,128)(2,1)} %broadcast_in_dim.24), calls=%async_computation.3 | async-start | bytes 1376256 | tf_op jit(solution)/shard_map/all_to_all | solution.py:16
  79.7 2.2 %copy-start = (bf16[512,448]{0,1:T(8,128)(2,1)S(1)}, bf16[512,448]{0,1:T(8,128)(2,1)}, u32[]{:S(2)}) copy-start(bf16[512,448]{0,1:T(8,128)(2,1)} %param.8) | copy-start | bytes 1376260
  79.7 2.2 %copy-start.1 = (bf16[512,448]{0,1:T(8,128)(2,1)S(1)}, bf16[512,448]{0,1:T(8,128)(2,1)}, u32[]{:S(2)}) copy-start(bf16[512,448]{0,1:T(8,128)(2,1)} %param.7) | copy-start | bytes 1376260
  98.9 5.5 %copy-start.2 = (bf16[256,512]{1,0:T(8,128)(2,1)S(1)}, bf16[256,512]{1,0:T(8,128)(2,1)}, u32[]{:S(2)}) copy-start(bf16[256,512]{1,0:T(8,128)(2,1)} %get-tuple-element.5) | copy-start | bytes 786436
  98.9 5.5 %copy-start.3 = (bf16[256,512]{1,0:T(8,128)(2,1)S(1)}, bf16[256,512]{1,0:T(8,128)(2,1)}, u32[]{:S(2)}) copy-start(bf16[256,512]{1,0:T(8,128)(2,1)} %get-tuple-element.6) | copy-start | bytes 786436
  100.4 16.2 %all-to-all-start.4 = ((bf16[32,8,1024]{2,1,0:T(8,128)(2,1)}), bf16[32,8,1024]{2,1,0:T(8,128)(2,1)S(1)}, u32[]{:S(2)}, u32[]{:S(2)}) async-start(bf16[32,8,1024]{2,1,0:T(8,128)(2,1)} %fusion), calls=%async_computation.4 | async-start | bytes 1048576 | tf_op jit(solution)/shard_map/all_to_all | solution.py:92
  104.3 8.9 %copy-start.4 = (bf16[256,512]{1,0:T(8,128)(2,1)S(1)}, bf16[256,512]{1,0:T(8,128)(2,1)}, u32[]{:S(2)}) copy-start(bf16[256,512]{1,0:T(8,128)(2,1)} %get-tuple-element.7) | copy-start | bytes 786436
  104.4 6.7 %collective-permute-start.2 = (bf16[256,1024]{1,0:T(8,128)(2,1)S(1)}, bf16[256,1024]{1,0:T(8,128)(2,1)S(1)}, u32[]{:S(2)}, u32[]{:S(2)}) collective-permute-start(bf16[256,1024]{1,0:T(8,128)(2,1)S(1)} %pad_maximum_fusion.2), channel_id=1, source_target_pairs={{0,1},{1,0},{2,3},{3,2},{4,5},{5,4},{6,7},{7,6},{8,9},{9,8},{10,11... | collective-permute-start | bytes 1572872 | tf_op jit(solution)/shard_map/ppermute | solution.py:101
  109.2 4.0 %collective-permute-start.3 = (bf16[3,448,256]{2,1,0:T(8,128)(2,1)S(1)}, bf16[3,448,256]{2,1,0:T(8,128)(2,1)S(1)}, u32[]{:S(2)}, u32[]{:S(2)}) collective-permute-start(bf16[3,448,256]{2,1,0:T(8,128)(2,1)S(1)} %bitcast.52), channel_id=1, source_target_pairs={{0,1},{1,0},{2,3},{3,2},{4,5},{5,4},{6,7},{7,6},{8,9},{9,8},{10,11... | collective-permute-start | bytes 2064392 | tf_op jit(solution)/shard_map/ppermute | solution.py:107
  116.7 8.5 %collective-permute-start.1 = (bf16[8,512]{1,0:T(8,128)(2,1)S(1)}, bf16[8,512]{1,0:T(8,128)(2,1)S(1)}, u32[]{:S(2)}, u32[]{:S(2)}) collective-permute-start(bf16[8,512]{1,0:T(8,128)(2,1)S(1)} %get-tuple-element.22), channel_id=1, source_target_pairs={{0,1},{1,0},{2,3},{3,2},{4,5},{5,4},{6,7},{7,6},{8,9},{9,8},{10,11... | collective-permute-start | bytes 24584 | tf_op jit(solution)/shard_map/ppermute | solution.py:94

commit v3 on v1

v3 whole, which is shorter than its diff:
```python
import jax
import jax.numpy as jnp
from jax import lax
from jax.experimental import pallas as pl
from jax.experimental.pallas import tpu as pltpu
from jax.sharding import Mesh
from jax.sharding import PartitionSpec as P

X, Y, Z = 4, 8, 8
ROW = ("x", "y")
COL = ("z", "core")
SWAP = ((0, 1), (1, 0))
PARAMS = pltpu.CompilerParams(vmem_limit_bytes=16 * 1024 * 1024)


def gather(block, axis, count):
    return lax.all_to_all(jnp.broadcast_to(block[None], (count,) + block.shape), axis, 0, 0)


def swiglu_parts(gate, up_val, hidden_grad):
    sigma = jax.nn.sigmoid(gate)
    hidden = (gate * sigma * up_val).astype(jnp.bfloat16)
    up_grad = (hidden_grad * gate * sigma).astype(jnp.bfloat16)
    gate_grad = (hidden_grad * up_val * sigma * (1.0 + gate * (1.0 - sigma))).astype(jnp.bfloat16)
    return jnp.stack([hidden, gate_grad, up_grad])


def product(a, b, contract_a, contract_b):
    return lax.dot_general(
        a, b, (((contract_a,), (contract_b,)), ((), ())), preferred_element_type=jnp.float32
    )


def cost(flops, bytes_accessed):
    return pl.CostEstimate(flops=flops, bytes_accessed=bytes_accessed, transcendentals=0)


def forward_kernel(mine_ref, other_ref, both_ref, out_ref):
    width = mine_ref.shape[2]
    rows = out_ref.shape[2]
    for i in range(3):
        at = i // 2 * width
        total = product(mine_ref[i], both_ref[:, at : at + width], 1, 1)
        at += 2 * width
        total = total + product(other_ref[i], both_ref[:, at : at + width], 1, 1)
        for part in range(out_ref.shape[0]):
            out_ref[part, i] = total[part * rows : (part + 1) * rows].astype(out_ref.dtype)


def forward(mine, other, both):
    _, units, width = mine.shape
    half = both.shape[0]
    whole = pl.BlockSpec(memory_space=pltpu.VMEM)
    return pl.pallas_call(
        forward_kernel,
        in_specs=[whole] * 3,
        out_specs=whole,
        out_shape=jax.ShapeDtypeStruct((Z, 3, units // Z, half), jnp.bfloat16),
        compiler_params=PARAMS,
        cost_estimate=cost(12 * units * width * half, 16 * units * width),
        name="forward",
    )(mine, other, both)


def backward_kernel(core_ref, mine_ref, other_ref, here_ref, there_ref, down_ref, gate_ref, up_ref):
    total = product(mine_ref[0], here_ref[...], 1, 0) + product(other_ref[0], there_ref[0], 1, 0)
    total = total.astype(jnp.bfloat16)
    for step, out_ref in enumerate((down_ref, gate_ref, up_ref)):

        @pl.when(pl.program_id(0) == step)
        def store(out_ref=out_ref):
            out_ref[...] = total


def backward(core, mine, other, both, others):
    _, units, half = mine.shape
    width = others.shape[2] // 2
    block = pl.BlockSpec((1, units, half), lambda i, core: (i, 0, 0))
    tokens = pl.BlockSpec((half, width), lambda i, core: (0, 1 - (i + 1) // 2))
    there = pl.BlockSpec(
        (1, half, width), lambda i, core: (1 - core[0], 0, 1 - (i + 1) // 2)
    )
    whole = jax.ShapeDtypeStruct((units, width), jnp.bfloat16)
    return pl.pallas_call(
        backward_kernel,
        grid_spec=pltpu.PrefetchScalarGridSpec(
            num_scalar_prefetch=1,
            grid=(3,),
            in_specs=[block, block, tokens, there],
            out_specs=[pl.BlockSpec((units, width), lambda i, core: (0, 0))] * 3,
        ),
        out_shape=[whole] * 3,
        compiler_params=PARAMS,
        cost_estimate=cost(12 * units * width * half, 16 * units * half),
        name="backward",
    )(core, mine, other, both, others)


def input_kernel(own_ref, mine_ref, other_ref, out_ref):
    width = mine_ref.shape[2]
    shape = out_ref.shape[:2] + (width,)
    for at, ref in ((0, mine_ref), (width, other_ref)):
        total = product(own_ref[1], ref[0], 0, 0) + product(own_ref[2], ref[1], 0, 0)
        out_ref[:, :, at : at + width] = total.reshape(shape).astype(out_ref.dtype)


def input_terms(own, mine, other):
    _, units, width = mine.shape
    half = own.shape[2]
    whole = pl.BlockSpec(memory_space=pltpu.VMEM)
    return pl.pallas_call(
        input_kernel,
        in_specs=[whole] * 3,
        out_specs=whole,
        out_shape=jax.ShapeDtypeStruct((X * Y, half // (X * Y), 2 * width), jnp.bfloat16),
        compiler_params=PARAMS,
        cost_estimate=cost(8 * units * width * half, 8 * units * width),
        name="input_terms",
    )(own, mine, other)


def on_device(activations, out_grad, w_gate, w_up, w_down):
    tokens, width = activations.shape
    units = w_gate.shape[1]
    few = tokens // 2
    half = X * Y * few
    rows = units // Z
    first = lax.axis_index("core") == 0

    sent = jnp.concatenate([activations, out_grad], axis=1).reshape(1, 2, few, 2 * width)
    sent = jnp.broadcast_to(sent, (Y, 2, few, 2 * width)).reshape(2 * Y, few, 2 * width)
    got = lax.all_to_all(sent, ("y", "core"), 0, 0).reshape(Y, 2, few, 2 * width)
    own = jnp.where(first, got[:, 0], got[:, 1])
    other = jnp.where(first, got[:, 1], got[:, 0])
    block = jnp.concatenate([own, other], axis=2).reshape(Y * few, 4 * width)
    both = gather(block, "x", X).reshape(half, 4 * width)

    weights = jnp.stack([w_gate.T, w_up.T, w_down])
    swapped = lax.ppermute(weights, "core", SWAP)

    sent = forward(weights, swapped, both)
    summed = jnp.sum(lax.all_to_all(sent, "z", 0, 0).astype(jnp.float32), axis=0)
    mine = swiglu_parts(summed[0], summed[1], summed[2])
    own = gather(mine, "z", Z).transpose(1, 0, 2, 3).reshape(3, units, half)

    term = input_terms(own, weights, swapped)
    terms = lax.all_to_all(term, ROW, 0, 0)
    total = jnp.sum(terms.astype(jnp.float32), axis=0).astype(jnp.bfloat16)
    pairs = lax.all_gather(total, "core", axis=0)
    in_grad = jnp.concatenate(
        [
            jnp.where(first, pairs[0, :, :width], pairs[0, :, width:]),
            jnp.where(first, pairs[1, :, width:], pairs[1, :, :width]),
        ]
    )


    others = jnp.concatenate(
        [
            lax.all_gather(both[:, 2 * width : 3 * width], "core", axis=0),
            lax.all_gather(both[:, 3 * width :], "core", axis=0),
        ],
        axis=2,
    )
    core = lax.axis_index("core").astype(jnp.int32).reshape(1)
    grad_down, grad_gate, grad_up = backward(core, own, lax.ppermute(own, "core", SWAP), both, others)
    grad_gate, grad_up = grad_gate.T, grad_up.T

    return (in_grad, grad_gate, grad_up, grad_down)


def solution(mesh):
    grid = Mesh(mesh.devices.reshape(X, Y, Z, 2), ROW + COL)
    return jax.shard_map(
        on_device,
        mesh=grid,
        in_specs=(P(ROW, COL), P(ROW, COL), P(COL, ROW), P(COL, ROW), P(ROW, COL)),
        out_specs=(P(ROW, COL), P(COL, ROW), P(COL, ROW), P(ROW, COL)),
        check_vma=False,
    )
```

time: 142 us -> 124 us (0.87)
  the two profiles are of different devices: /device:TPU:8 before, /device:TPU:1 now
where the time goes in v3:
time: 124 us; the launch traced here: 123 us
  blocking collectives  78 us (63%)
  starting transfers between devices  22.8 us (18%)
  waiting for transfers between devices  8.27 us (7%)
  Pallas kernels  6.93 us (6%)
  other arithmetic  4.26 us (3%)
  local copies, waits for them, and re-layouts  1.76 us (1%)
    all_to_all x2, blocking collectives, gather(): lax.all_to_all(jnp.broadcast_to(block[None], (count,) + block.shape), axi...  38.7 us
    all_to_all x1, blocking collectives, on_device(): lax.all_to_all(sent, 'z', 0, 0).astype(jnp.float32)  28.8 us
    all_to_all x1, starting transfers between devices, on_device(): lax.all_to_all(sent, ('y', 'core'), 0, 0).reshape(Y, 2, few, 2 * width)  10.2 us
    all_to_all x1, waiting for transfers between devices, on_device(): lax.all_to_all(sent, ('y', 'core'), 0, 0).reshape(Y, 2, few, 2 * width)  8.26 us
    all_gather x1, blocking collectives, on_device(): pairs = lax.all_gather(total, 'core', axis=0)  6.14 us
    ppermute x1, starting transfers between devices, on_device(): lax.ppermute(own, 'core', SWAP)  5.83 us
    all_to_all x1, starting transfers between devices, on_device(): terms = lax.all_to_all(term, ROW, 0, 0)  4.62 us
    pallas_call x1, Pallas kernels, backward(): pl.pallas_call(backward_kernel, grid_spec=pltpu.PrefetchScalarGridSpec(nu...  2.61 us
  transfers between devices with their start and end apart: 4, of which 1 were waited for; matrix products, arithmetic and copies ran while one was open for 1% of the time, Pallas kernels for 2%

profile of v3, /device:TPU:1, one launch (start us, length us, event | category | flops | bytes accessed | tf_op | source)
XLA Modules:
  0.0 122.8 jit_solution(17659705215271659880)
XLA Ops:
  0.6 0.7 maximum_bitcast_fusion.1
  1.4 0.7 broadcast_in_dim.21
  2.1 10.2 %all-to-all-start = ((bf16[16,8,1024]{2,1,0:T(8,128)(2,1)}), bf16[16,8,1024]{2,1,0:T(8,128)(2,1)S(1)}, u32[]{:S(2)}, u32[]{:S(2)}) async-start(bf16[16,8,1024]{2,1,0:T(8,128)(2,1)} %bitcast.6), calls=%async_computation | async-start | bytes 524288 | tf_op jit(solution)/shard_map/all_to_all | solution.py:132
  12.3 1.4 %pad_maximum_fusion.mine_ref = bf16[3,448,512]{2,1,0:T(8,128)(2,1)S(1)} fusion(bf16[1,448,512]{2,1,0:T(8,128)(2,1)} %bitcast.40, bf16[1,448,512]{2,1,0:T(8,128)(2,1)} %bitcast.41, bf16[1,448,512]{2,1,0:T(8,128)(2,1)} %bitcast.42), kind=kLoop, calls=%fused_computation | loop fusion | flops 1376256 | bytes 2752512 | tf_op jit(solution)/shard_map/stack | solution.py:138
  13.7 2.1 %collective-permute-start = (bf16[3,448,512]{2,1,0:T(8,128)(2,1)S(1)}, bf16[3,448,512]{2,1,0:T(8,128)(2,1)}, u32[]{:S(2)}, u32[]{:S(2)}) collective-permute-start(bf16[3,448,512]{2,1,0:T(8,128)(2,1)S(1)} %pad_maximum_fusion.mine_ref), channel_id=1, source_target_pairs={{0,1},{1,0},{2,3},{3,2},{4,5},{5,4},{6,7},{7,6},{8,9},{9,8},{10,11... | collective-permute-start | bytes 4128776 | tf_op jit(solution)/shard_map/ppermute | solution.py:139
  15.9 8.3 %all-to-all-done = bf16[16,8,1024]{2,1,0:T(8,128)(2,1)S(1)} async-done(((bf16[16,8,1024]{2,1,0:T(8,128)(2,1)}), bf16[16,8,1024]{2,1,0:T(8,128)(2,1)S(1)}, u32[]{:S(2)}, u32[]{:S(2)}) %all-to-all-start) | async-done | bytes 262176 | tf_op jit(solution)/shard_map/all_to_all | solution.py:132
  24.2 0.1 broadcast_in_dim.23
  24.3 18.0 %all_to_all.25 = bf16[4,64,2048]{2,1,0:T(8,128)(2,1)S(1)} all-to-all(bf16[4,64,2048]{2,1,0:T(8,128)(2,1)S(1)} %broadcast_in_dim.23), channel_id=1, replica_groups=mesh['x'=4,'y'=8,'z'=8,'core'=2] {'x'}, dimensions={0} | all-to-all | bytes 2097152 | tf_op jit(solution)/shard_map/all_to_all | solution.py:17
  42.3 0.0 collective-permute-done.other_ref
  42.3 2.2 %forward.1 = bf16[8,3,56,256]{3,2,1,0:T(8,128)(2,1)S(1)} custom-call(bf16[3,448,512]{2,1,0:T(8,128)(2,1)S(1)} %pad_maximum_fusion.mine_ref, bf16[3,448,512]{2,1,0:T(8,128)(2,1)} %collective-permute-done.other_ref, bf16[256,2048]{1,0:T(8,128)(2,1)S(1)} %bitcast.30), custom_call_target="tpu_custom_call" | custom-call | flops 704643072 | bytes 3670016 | tf_op jit(solution)/shard_map/forward/pallas_call | solution.py:54
  44.6 28.8 %all_to_all.26 = bf16[8,3,56,256]{3,2,1,0:T(8,128)(2,1)S(1)} all-to-all(bf16[8,3,56,256]{3,2,1,0:T(8,128)(2,1)S(1)} %forward.1), channel_id=1, replica_groups=mesh['x'=4,'y'=8,'z'=8,'core'=2] {'z'}, dimensions={0} | all-to-all | bytes 1376256 | tf_op jit(solution)/shard_map/all_to_all | solution.py:142
  73.4 0.1 convert_reduce_fusion
  73.6 20.7 %all_to_all.27 = bf16[8,3,56,256]{3,2,1,0:T(8,128)(2,1)S(1)} all-to-all(bf16[8,3,56,256]{3,2,1,0:T(8,128)(2,1)S(1)} %broadcast_in_dim.24), channel_id=1, replica_groups=mesh['x'=4,'y'=8,'z'=8,'core'=2] {'z'}, dimensions={0} | all-to-all | bytes 1376256 | tf_op jit(solution)/shard_map/all_to_all | solution.py:17
  94.4 2.1 %input_terms.1 = bf16[32,8,1024]{2,1,0:T(8,128)(2,1)S(1)} custom-call(bf16[3,448,256]{2,1,0:T(8,128)(2,1)S(1)} %bitcast.33, bf16[3,448,512]{2,1,0:T(8,128)(2,1)S(1)} %pad_maximum_fusion.mine_ref, bf16[3,448,512]{2,1,0:T(8,128)(2,1)} %collective-permute-done.other_ref), custom_call_target="tpu_custom_call" | custom-call | flops 469762048 | bytes 1835008 | tf_op jit(solution)/shard_map/input_terms/pallas_call | solution.py:111
  96.5 0.0 copy-start
  96.5 0.8 copy-done
  97.3 4.6 %all-to-all-start.4 = ((bf16[32,8,1024]{2,1,0:T(8,128)(2,1)}), bf16[32,8,1024]{2,1,0:T(8,128)(2,1)}, u32[]{:S(2)}, u32[]{:S(2)}) async-start(bf16[32,8,1024]{2,1,0:T(8,128)(2,1)} %copy-done), calls=%async_computation.4 | async-start | bytes 1048576 | tf_op jit(solution)/shard_map/all_to_all | solution.py:147
  101.9 5.8 %collective-permute-start.1 = (bf16[3,448,256]{2,1,0:T(8,128)(2,1)S(1)}, bf16[3,448,256]{2,1,0:T(8,128)(2,1)S(1)}, u32[]{:S(2)}, u32[]{:S(2)}) collective-permute-start(bf16[3,448,256]{2,1,0:T(8,128)(2,1)S(1)} %bitcast.34), channel_id=1, source_target_pairs={{0,1},{1,0},{2,3},{3,2},{4,5},{5,4},{6,7},{7,6},{8,9},{9,8},{10,11... | collective-permute-start | bytes 2064392 | tf_op jit(solution)/shard_map/ppermute | solution.py:166
  107.8 2.2 %all-gather.2 = bf16[512,512]{1,0:T(8,128)(2,1)S(1)} all-gather(bf16[256,512]{1,0:T(8,128)(2,1)S(1)} %get-tuple-element.11), channel_id=4, replica_groups=mesh['x'=4,'y'=8,'z'=8,'core'=2] {'core'}, dimensions={0}, use_global_device_ids=true | all-gather | bytes 786432 | tf_op jit(solution)/shard_map/all_gather | solution.py:161
  110.0 2.2 %all-gather.1 = bf16[512,512]{1,0:T(8,128)(2,1)S(1)} all-gather(bf16[256,512]{1,0:T(8,128)(2,1)S(1)} %get-tuple-element.10), channel_id=3, replica_groups=mesh['x'=4,'y'=8,'z'=8,'core'=2] {'core'}, dimensions={0}, use_global_device_ids=true | all-gather | bytes 786432 | tf_op jit(solution)/shard_map/all_gather | solution.py:160
  112.1 0.1 pad_maximum_fusion.1.there_ref
  112.3 0.0 collective-permute-done.1.other_ref
  112.3 2.6 %backward.1 = (bf16[448,512]{1,0:T(8,128)(2,1)}, bf16[448,512]{1,0:T(8,128)(2,1)}, bf16[448,512]{1,0:T(8,128)(2,1)}) custom-call(s32[1]{0:T(128)} %bitcast.17.core_ref, bf16[3,448,256]{2,1,0:T(8,128)(2,1)S(1)} %bitcast.35, bf16[3,448,256]{2,1,0:T(8,128)(2,1)S(1)} %collective-permute-done.1.other_ref, bf16[256,2048]{1,0:T(8,128)(2,1)S(1)} %bitcast.32, ...), custom_call_target="tpu_custom_call" | custom-call | flops 704643072 | bytes 1835008 | tf_op jit(solution)/shard_map/backward/pallas_call | solution.py:84
  114.9 0.0 all-to-all-done.4
  114.9 1.1 reduce_sum.22
  116.1 6.1 %all-gather = bf16[16,1024]{1,0:T(8,128)(2,1)S(1)} all-gather(bf16[8,1024]{1,0:T(8,128)(2,1)S(1)} %reduce_sum.22), channel_id=2, replica_groups=mesh['x'=4,'y'=8,'z'=8,'core'=2] {'core'}, dimensions={0}, use_global_device_ids=true | all-gather | bytes 49152 | tf_op jit(solution)/shard_map/all_gather | solution.py:149
  122.2 0.6 pad_maximum_fusion.3
  (8 shorter events, 0.2 us)
Async XLA Ops:
  2.1 22.1 %all-to-all-start = ((bf16[16,8,1024]{2,1,0:T(8,128)(2,1)}), bf16[16,8,1024]{2,1,0:T(8,128)(2,1)S(1)}, u32[]{:S(2)}, u32[]{:S(2)}) async-start(bf16[16,8,1024]{2,1,0:T(8,128)(2,1)} %bitcast.6), calls=%async_computation | async-start | bytes 524288 | tf_op jit(solution)/shard_map/all_to_all | solution.py:132
  13.7 28.6 %collective-permute-start = (bf16[3,448,512]{2,1,0:T(8,128)(2,1)S(1)}, bf16[3,448,512]{2,1,0:T(8,128)(2,1)}, u32[]{:S(2)}, u32[]{:S(2)}) collective-permute-start(bf16[3,448,512]{2,1,0:T(8,128)(2,1)S(1)} %pad_maximum_fusion.mine_ref), channel_id=1, source_target_pairs={{0,1},{1,0},{2,3},{3,2},{4,5},{5,4},{6,7},{7,6},{8,9},{9,8},{10,11... | collective-permute-start | bytes 4128776 | tf_op jit(solution)/shard_map/ppermute | solution.py:139
  96.5 0.8 copy-start
  97.3 17.6 %all-to-all-start.4 = ((bf16[32,8,1024]{2,1,0:T(8,128)(2,1)}), bf16[32,8,1024]{2,1,0:T(8,128)(2,1)}, u32[]{:S(2)}, u32[]{:S(2)}) async-start(bf16[32,8,1024]{2,1,0:T(8,128)(2,1)} %copy-done), calls=%async_computation.4 | async-start | bytes 1048576 | tf_op jit(solution)/shard_map/all_to_all | solution.py:147
  101.9 10.4 %collective-permute-start.1 = (bf16[3,448,256]{2,1,0:T(8,128)(2,1)S(1)}, bf16[3,448,256]{2,1,0:T(8,128)(2,1)S(1)}, u32[]{:S(2)}, u32[]{:S(2)}) collective-permute-start(bf16[3,448,256]{2,1,0:T(8,128)(2,1)S(1)} %bitcast.34), channel_id=1, source_target_pairs={{0,1},{1,0},{2,3},{3,2},{4,5},{5,4},{6,7},{7,6},{8,9},{9,8},{10,11... | collective-permute-start | bytes 2064392 | tf_op jit(solution)/shard_map/ppermute | solution.py:166

commit v4 on v3

--- a/solution.py
+++ b/solution.py
@@ -35,31 +35,32 @@
     return pl.CostEstimate(flops=flops, bytes_accessed=bytes_accessed, transcendentals=0)
 
 
-def forward_kernel(mine_ref, other_ref, both_ref, out_ref):
-    width = mine_ref.shape[2]
+def forward_kernel(core_ref, gate_ref, up_ref, down_ref, both_ref, out_ref):
+    core = core_ref[0]
+    width = gate_ref.shape[2]
     rows = out_ref.shape[2]
-    for i in range(3):
+    for i, ref in enumerate((gate_ref, up_ref, down_ref)):
         at = i // 2 * width
-        total = product(mine_ref[i], both_ref[:, at : at + width], 1, 1)
+        total = product(ref[core], both_ref[:, at : at + width], 1, 1)
         at += 2 * width
-        total = total + product(other_ref[i], both_ref[:, at : at + width], 1, 1)
+        total = total + product(ref[1 - core], both_ref[:, at : at + width], 1, 1)
         for part in range(out_ref.shape[0]):
             out_ref[part, i] = total[part * rows : (part + 1) * rows].astype(out_ref.dtype)
 
 
-def forward(mine, other, both):
-    _, units, width = mine.shape
+def forward(core, weights, both):
+    _, units, width = weights[0].shape
     half = both.shape[0]
     whole = pl.BlockSpec(memory_space=pltpu.VMEM)
     return pl.pallas_call(
         forward_kernel,
-        in_specs=[whole] * 3,
+        in_specs=[pl.BlockSpec(memory_space=pltpu.SMEM)] + [whole] * 4,
         out_specs=whole,
         out_shape=jax.ShapeDtypeStruct((Z, 3, units // Z, half), jnp.bfloat16),
         compiler_params=PARAMS,
         cost_estimate=cost(12 * units * width * half, 16 * units * width),
         name="forward",
-    )(mine, other, both)
+    )(core, *weights, both)
 
 
 def backward_kernel(core_ref, mine_ref, other_ref, here_ref, there_ref, down_ref, gate_ref, up_ref):
@@ -96,27 +97,39 @@
     )(core, mine, other, both, others)
 
 
-def input_kernel(own_ref, mine_ref, other_ref, out_ref):
-    width = mine_ref.shape[2]
-    shape = out_ref.shape[:2] + (width,)
-    for at, ref in ((0, mine_ref), (width, other_ref)):
-        total = product(own_ref[1], ref[0], 0, 0) + product(own_ref[2], ref[1], 0, 0)
-        out_ref[:, :, at : at + width] = total.reshape(shape).astype(out_ref.dtype)
+def input_kernel(core_ref, own_ref, gate_ref, up_ref, out_ref, block_ref, sent_ref):
+    core = core_ref[0]
+    width = gate_ref.shape[2]
+    copies = []
+    for i, side in enumerate((core, 1 - core)):
+        total = product(own_ref[1], gate_ref[side], 0, 0) + product(own_ref[2], up_ref[side], 0, 0)
+        block_ref[i] = total.astype(block_ref.dtype)
+        lanes = pl.ds(i * width, width)
+        copies.append(
+            pltpu.make_async_copy(block_ref.at[i], out_ref.at[:, lanes], sent_ref.at[i])
+        )
+        copies[i].start()
+    for copy in copies:
+        copy.wait()
 
 
-def input_terms(own, mine, other):
-    _, units, width = mine.shape
+def input_terms(core, own, weights):
+    _, units, width = weights[0].shape
     half = own.shape[2]
     whole = pl.BlockSpec(memory_space=pltpu.VMEM)
     return pl.pallas_call(
         input_kernel,
-        in_specs=[whole] * 3,
-        out_specs=whole,
-        out_shape=jax.ShapeDtypeStruct((X * Y, half // (X * Y), 2 * width), jnp.bfloat16),
+        in_specs=[pl.BlockSpec(memory_space=pltpu.SMEM)] + [whole] * 3,
+        out_specs=pl.BlockSpec(memory_space=pltpu.HBM),
+        out_shape=jax.ShapeDtypeStruct((half, 2 * width), jnp.bfloat16),
+        scratch_shapes=[
+            pltpu.VMEM((2, half, width), jnp.bfloat16),
+            pltpu.SemaphoreType.DMA((2,)),
+        ],
         compiler_params=PARAMS,
         cost_estimate=cost(8 * units * width * half, 8 * units * width),
         name="input_terms",
-    )(own, mine, other)
+    )(core, own, *weights[:2])
 
 
 def on_device(activations, out_grad, w_gate, w_up, w_down):
@@ -133,18 +146,18 @@
     own = jnp.where(first, got[:, 0], got[:, 1])
     other = jnp.where(first, got[:, 1], got[:, 0])
     block = jnp.concatenate([own, other], axis=2).reshape(Y * few, 4 * width)
+    core = lax.axis_index("core").astype(jnp.int32).reshape(1)
+    weights = [lax.all_gather(w, "core", axis=0) for w in (w_gate.T, w_up.T, w_down)]
+    block, weights = lax.optimization_barrier((block, weights))
     both = gather(block, "x", X).reshape(half, 4 * width)
 
-    weights = jnp.stack([w_gate.T, w_up.T, w_down])
-    swapped = lax.ppermute(weights, "core", SWAP)
-
-    sent = forward(weights, swapped, both)
+    sent = forward(core, weights, both)
     summed = jnp.sum(lax.all_to_all(sent, "z", 0, 0).astype(jnp.float32), axis=0)
     mine = swiglu_parts(summed[0], summed[1], summed[2])
     own = gather(mine, "z", Z).transpose(1, 0, 2, 3).reshape(3, units, half)
 
-    term = input_terms(own, weights, swapped)
-    terms = lax.all_to_all(term, ROW, 0, 0)
+    term = input_terms(core, own, weights)
+    terms = lax.all_to_all(term.reshape(X * Y, few, 2 * width), ROW, 0, 0)
     total = jnp.sum(terms.astype(jnp.float32), axis=0).astype(jnp.bfloat16)
     pairs = lax.all_gather(total, "core", axis=0)
     in_grad = jnp.concatenate(
@@ -162,7 +175,6 @@
         ],
         axis=2,
     )
-    core = lax.axis_index("core").astype(jnp.int32).reshape(1)
     grad_down, grad_gate, grad_up = backward(core, own, lax.ppermute(own, "core", SWAP), both, others)
     grad_gate, grad_up = grad_gate.T, grad_up.T
 

time: 124 us -> 120 us (0.968)
  blocking collectives: 78 us -> 85.8 us
  waiting for transfers between devices: 8.27 us -> 4.22 us
  starting transfers between devices: 22.8 us -> 20.1 us
  other arithmetic: 4.26 us -> 1.82 us
  Pallas kernels: 6.93 us -> 5.02 us
    all_gather x0 -> x3, blocking collectives: none -> 7.63 us  [on_device(): lax.all_gather(w, 'core', axis=0)]
    all_to_all x1, waiting for transfers between devices: 8.26 us -> 4.22 us  [on_device(): lax.all_to_all(sent, ('y', 'core'), 0, 0).reshape(Y, 2, few, 2 * width)]
    ppermute x1 -> x0, starting transfers between devices: 2.13 us -> none  [on_device(): swapped = lax.ppermute(weights, 'core', SWAP)]
    pallas_call x2, Pallas kernels: 4.32 us -> 2.4 us  [the longest x1 1.49 us: input_terms(): pl.pallas_call(input_kernel, in_specs=[pl.BlockSpec(memory_space=pltpu.SM...]
    another operation x1 -> x0, other arithmetic: 1.44 us -> none  [on_device(): weights = jnp.stack([w_gate.T, w_up.T, w_down])]
  transfers between devices with their start and end apart: 4 -> 3, of which waited for: 1 -> 1; matrix products, arithmetic and copies ran while one was open for 1% -> 0% of each run, Pallas kernels for 2% -> 2%
where the time goes in v4:
time: 120 us; the launch traced here: 119 us
  blocking collectives  85.8 us (72%)
  starting transfers between devices  20.1 us (17%)
  Pallas kernels  5.02 us (4%)
  waiting for transfers between devices  4.22 us (4%)
  other arithmetic  1.82 us (2%)
    all_to_all x2, blocking collectives, gather(): lax.all_to_all(jnp.broadcast_to(block[None], (count,) + block.shape), axi...  38.9 us
    all_to_all x1, blocking collectives, on_device(): lax.all_to_all(sent, 'z', 0, 0).astype(jnp.float32)  28.8 us
    all_to_all x1, starting transfers between devices, on_device(): lax.all_to_all(sent, ('y', 'core'), 0, 0).reshape(Y, 2, few, 2 * width)  10.2 us
    all_gather x3, blocking collectives, on_device(): lax.all_gather(w, 'core', axis=0)  7.63 us
    all_gather x1, blocking collectives, on_device(): pairs = lax.all_gather(total, 'core', axis=0)  6.17 us
    ppermute x1, starting transfers between devices, on_device(): lax.ppermute(own, 'core', SWAP)  5.83 us
    all_to_all x1, waiting for transfers between devices, on_device(): lax.all_to_all(sent, ('y', 'core'), 0, 0).reshape(Y, 2, few, 2 * width)  4.22 us
    all_to_all x1, starting transfers between devices, on_device(): terms = lax.all_to_all(term.reshape(X * Y, few, 2 * width), ROW, 0, 0)  4.03 us
  transfers between devices with their start and end apart: 3, of which 1 were waited for; matrix products, arithmetic and copies ran while one was open for 0% of the time, Pallas kernels for 2%

profile of v4, /device:TPU:1, one launch (start us, length us, event | category | flops | bytes accessed | tf_op | source)
XLA Modules:
  0.0 118.7 jit_solution(13484239003089795628)
XLA Ops:
  0.6 0.0 copy-start.3
  0.6 0.8 maximum_bitcast_fusion
  1.4 0.7 broadcast_in_dim.9
  2.2 10.2 %all-to-all-start = ((bf16[16,8,1024]{2,1,0:T(8,128)(2,1)}), bf16[16,8,1024]{2,1,0:T(8,128)(2,1)S(1)}, u32[]{:S(2)}, u32[]{:S(2)}) async-start(bf16[16,8,1024]{2,1,0:T(8,128)(2,1)} %bitcast.2), calls=%async_computation | async-start | bytes 524288 | tf_op jit(solution)/shard_map/all_to_all | solution.py:145
  12.4 0.0 copy-done.3
  12.4 2.5 %all-gather = bf16[896,512]{1,0:T(8,128)(2,1)S(1)} all-gather(bf16[448,512]{1,0:T(8,128)(2,1)S(1)} %bitcast.42), channel_id=2, replica_groups=mesh['x'=4,'y'=8,'z'=8,'core'=2] {'core'}, dimensions={0}, use_global_device_ids=true | all-gather | bytes 1376256 | tf_op jit(solution)/shard_map/all_gather | solution.py:150
  14.8 0.0 copy-done.4
  14.8 2.6 %all-gather.1 = bf16[896,512]{1,0:T(8,128)(2,1)S(1)} all-gather(bf16[448,512]{1,0:T(8,128)(2,1)S(1)} %bitcast.43), channel_id=3, replica_groups=mesh['x'=4,'y'=8,'z'=8,'core'=2] {'core'}, dimensions={0}, use_global_device_ids=true | all-gather | bytes 1376256 | tf_op jit(solution)/shard_map/all_gather | solution.py:150
  17.4 0.0 copy-done.5
  17.4 2.6 %all-gather.2 = bf16[896,512]{1,0:T(8,128)(2,1)} all-gather(bf16[448,512]{1,0:T(8,128)(2,1)S(1)} %copy-done.5), channel_id=4, replica_groups=mesh['x'=4,'y'=8,'z'=8,'core'=2] {'core'}, dimensions={0}, use_global_device_ids=true | all-gather | bytes 1376256 | tf_op jit(solution)/shard_map/all_gather | solution.py:150
  20.0 4.2 %all-to-all-done = bf16[16,8,1024]{2,1,0:T(8,128)(2,1)S(1)} async-done(((bf16[16,8,1024]{2,1,0:T(8,128)(2,1)}), bf16[16,8,1024]{2,1,0:T(8,128)(2,1)S(1)}, u32[]{:S(2)}, u32[]{:S(2)}) %all-to-all-start) | async-done | bytes 262176 | tf_op jit(solution)/shard_map/all_to_all | solution.py:145
  24.3 0.1 broadcast_in_dim.10
  24.4 0.0 copy-start.2
  24.4 18.1 %all_to_all.25 = bf16[4,64,2048]{2,1,0:T(8,128)(2,1)S(1)} all-to-all(bf16[4,64,2048]{2,1,0:T(8,128)(2,1)S(1)} %broadcast_in_dim.10), channel_id=1, replica_groups=mesh['x'=4,'y'=8,'z'=8,'core'=2] {'x'}, dimensions={0} | all-to-all | bytes 2097152 | tf_op jit(solution)/shard_map/all_to_all | solution.py:17
  42.6 0.0 copy-done.2
  42.6 0.9 forward.1
  43.5 28.8 %all_to_all.26 = bf16[8,3,56,256]{3,2,1,0:T(8,128)(2,1)S(1)} all-to-all(bf16[8,3,56,256]{3,2,1,0:T(8,128)(2,1)S(1)} %forward.1), channel_id=1, replica_groups=mesh['x'=4,'y'=8,'z'=8,'core'=2] {'z'}, dimensions={0} | all-to-all | bytes 1376256 | tf_op jit(solution)/shard_map/all_to_all | solution.py:155
  72.3 0.1 convert_reduce_fusion
  72.5 20.7 %all_to_all.27 = bf16[8,3,56,256]{3,2,1,0:T(8,128)(2,1)S(1)} all-to-all(bf16[8,3,56,256]{3,2,1,0:T(8,128)(2,1)S(1)} %broadcast_in_dim.22), channel_id=1, replica_groups=mesh['x'=4,'y'=8,'z'=8,'core'=2] {'z'}, dimensions={0} | all-to-all | bytes 1376256 | tf_op jit(solution)/shard_map/all_to_all | solution.py:17
  93.3 0.0 copy-start
  93.3 1.5 %input_terms.1 = bf16[256,1024]{1,0:T(8,128)(2,1)} custom-call(s32[1]{0:T(128)} %bitcast.core_ref, bf16[3,448,256]{2,1,0:T(8,128)(2,1)S(1)} %bitcast.34, bf16[2,448,512]{2,1,0:T(8,128)(2,1)S(1)} %bitcast.31, bf16[2,448,512]{2,1,0:T(8,128)(2,1)S(1)} %bitcast.33), custom_call_target="tpu_custom_call" | custom-call | flops 469762048 | bytes 1835008 | tf_op jit(solution)/shard_map/input_terms/pallas_call | solution.py:120
  94.8 4.0 %all-to-all-start.4 = ((bf16[32,8,1024]{2,1,0:T(8,128)(2,1)}), bf16[32,8,1024]{2,1,0:T(8,128)(2,1)S(1)}, u32[]{:S(2)}, u32[]{:S(2)}) async-start(bf16[32,8,1024]{2,1,0:T(8,128)(2,1)} %bitcast.14), calls=%async_computation.4 | async-start | bytes 1048576 | tf_op jit(solution)/shard_map/all_to_all | solution.py:160
  98.9 5.8 %collective-permute-start = (bf16[3,448,256]{2,1,0:T(8,128)(2,1)S(1)}, bf16[3,448,256]{2,1,0:T(8,128)(2,1)S(1)}, u32[]{:S(2)}, u32[]{:S(2)}) collective-permute-start(bf16[3,448,256]{2,1,0:T(8,128)(2,1)S(1)} %bitcast.35), channel_id=1, source_target_pairs={{0,1},{1,0},{2,3},{3,2},{4,5},{5,4},{6,7},{7,6},{8,9},{9,8},{10,11... | collective-permute-start | bytes 2064392 | tf_op jit(solution)/shard_map/ppermute | solution.py:178
  104.7 2.2 %all-gather.5 = bf16[512,512]{1,0:T(8,128)(2,1)S(1)} all-gather(bf16[256,512]{1,0:T(8,128)(2,1)S(1)} %get-tuple-element.19), channel_id=7, replica_groups=mesh['x'=4,'y'=8,'z'=8,'core'=2] {'core'}, dimensions={0}, use_global_device_ids=true | all-gather | bytes 786432 | tf_op jit(solution)/shard_map/all_gather | solution.py:174
  106.9 2.2 %all-gather.4 = bf16[512,512]{1,0:T(8,128)(2,1)S(1)} all-gather(bf16[256,512]{1,0:T(8,128)(2,1)S(1)} %get-tuple-element.18), channel_id=6, replica_groups=mesh['x'=4,'y'=8,'z'=8,'core'=2] {'core'}, dimensions={0}, use_global_device_ids=true | all-gather | bytes 786432 | tf_op jit(solution)/shard_map/all_gather | solution.py:173
  109.1 0.1 pad_maximum_fusion.there_ref
  109.2 0.0 collective-permute-done.other_ref
  109.2 2.6 %backward.1 = (bf16[448,512]{1,0:T(8,128)(2,1)}, bf16[448,512]{1,0:T(8,128)(2,1)}, bf16[448,512]{1,0:T(8,128)(2,1)}) custom-call(s32[1]{0:T(128)} %bitcast.core_ref, bf16[3,448,256]{2,1,0:T(8,128)(2,1)S(1)} %bitcast.36, bf16[3,448,256]{2,1,0:T(8,128)(2,1)S(1)} %collective-permute-done.other_ref, bf16[256,2048]{1,0:T(8,128)(2,1)S(1)} %bitcast.29, ...), custom_call_target="tpu_custom_call" | custom-call | flops 704643072 | bytes 1835008 | tf_op jit(solution)/shard_map/backward/pallas_call | solution.py:85
  111.9 0.0 all-to-all-done.4
  111.9 0.1 reduce_sum.22
  111.9 6.2 %all-gather.3 = bf16[16,1024]{1,0:T(8,128)(2,1)S(1)} all-gather(bf16[8,1024]{1,0:T(8,128)(2,1)S(1)} %reduce_sum.22), channel_id=5, replica_groups=mesh['x'=4,'y'=8,'z'=8,'core'=2] {'core'}, dimensions={0}, use_global_device_ids=true | all-gather | bytes 49152 | tf_op jit(solution)/shard_map/all_gather | solution.py:162
  118.1 0.6 pad_maximum_fusion.3
  (13 shorter events, 0.2 us)
Async XLA Ops:
  0.6 11.7 %copy-start.3 = (bf16[512,448]{0,1:T(8,128)(2,1)S(1)}, bf16[512,448]{0,1:T(8,128)(2,1)}, u32[]{:S(2)}) copy-start(bf16[512,448]{0,1:T(8,128)(2,1)} %param.7) | copy-start | bytes 1376260
  1.4 13.4 %copy-start.4 = (bf16[512,448]{0,1:T(8,128)(2,1)S(1)}, bf16[512,448]{0,1:T(8,128)(2,1)}, u32[]{:S(2)}) copy-start(bf16[512,448]{0,1:T(8,128)(2,1)} %param.8) | copy-start | bytes 1376260
  2.2 22.1 %all-to-all-start = ((bf16[16,8,1024]{2,1,0:T(8,128)(2,1)}), bf16[16,8,1024]{2,1,0:T(8,128)(2,1)S(1)}, u32[]{:S(2)}, u32[]{:S(2)}) async-start(bf16[16,8,1024]{2,1,0:T(8,128)(2,1)} %bitcast.2), calls=%async_computation | async-start | bytes 524288 | tf_op jit(solution)/shard_map/all_to_all | solution.py:145
  14.8 2.6 %copy-start.5 = (bf16[448,512]{1,0:T(8,128)(2,1)S(1)}, bf16[448,512]{1,0:T(8,128)(2,1)}, u32[]{:S(2)}) copy-start(bf16[448,512]{1,0:T(8,128)(2,1)} %param.9) | copy-start | bytes 1376260
  24.4 18.2 %copy-start.2 = (bf16[896,512]{1,0:T(8,128)(2,1)S(1)}, bf16[896,512]{1,0:T(8,128)(2,1)}, u32[]{:S(2)}) copy-start(bf16[896,512]{1,0:T(8,128)(2,1)} %all-gather.2) | copy-start | bytes 2752516
  93.3 1.5 %copy-start = (bf16[3,8,56,256]{3,2,1,0:T(8,128)(2,1)}, bf16[3,8,56,256]{3,2,1,0:T(8,128)(2,1)S(1)}, u32[]{:S(2)}) copy-start(bf16[3,8,56,256]{3,2,1,0:T(8,128)(2,1)S(1)} %copy.9) | copy-start | bytes 2064388
  94.8 4.1 %copy-start.1 = (bf16[3,8,56,256]{3,2,1,0:T(8,128)(2,1)S(1)}, bf16[3,8,56,256]{3,2,1,0:T(8,128)(2,1)}, u32[]{:S(2)}) copy-start(bf16[3,8,56,256]{3,2,1,0:T(8,128)(2,1)} %copy-done) | copy-start | bytes 2064388
  94.8 17.1 %all-to-all-start.4 = ((bf16[32,8,1024]{2,1,0:T(8,128)(2,1)}), bf16[32,8,1024]{2,1,0:T(8,128)(2,1)S(1)}, u32[]{:S(2)}, u32[]{:S(2)}) async-start(bf16[32,8,1024]{2,1,0:T(8,128)(2,1)} %bitcast.14), calls=%async_computation.4 | async-start | bytes 1048576 | tf_op jit(solution)/shard_map/all_to_all | solution.py:160
  98.9 10.4 %collective-permute-start = (bf16[3,448,256]{2,1,0:T(8,128)(2,1)S(1)}, bf16[3,448,256]{2,1,0:T(8,128)(2,1)S(1)}, u32[]{:S(2)}, u32[]{:S(2)}) collective-permute-start(bf16[3,448,256]{2,1,0:T(8,128)(2,1)S(1)} %bitcast.35), channel_id=1, source_target_pairs={{0,1},{1,0},{2,3},{3,2},{4,5},{5,4},{6,7},{7,6},{8,9},{9,8},{10,11... | collective-permute-start | bytes 2064392 | tf_op jit(solution)/shard_map/ppermute | solution.py:178

commit v5 on v4

--- a/solution.py
+++ b/solution.py
@@ -140,11 +140,11 @@
     rows = units // Z
     first = lax.axis_index("core") == 0
 
-    sent = jnp.concatenate([activations, out_grad], axis=1).reshape(1, 2, few, 2 * width)
-    sent = jnp.broadcast_to(sent, (Y, 2, few, 2 * width)).reshape(2 * Y, few, 2 * width)
-    got = lax.all_to_all(sent, ("y", "core"), 0, 0).reshape(Y, 2, few, 2 * width)
-    own = jnp.where(first, got[:, 0], got[:, 1])
-    other = jnp.where(first, got[:, 1], got[:, 0])
+    sent = jnp.concatenate([activations, out_grad], axis=1).reshape(2, 1, few, 2 * width)
+    sent = jnp.broadcast_to(sent, (2, Y, few, 2 * width)).reshape(2 * Y, few, 2 * width)
+    got = lax.all_to_all(sent, ("core", "y"), 0, 0).reshape(2, Y, few, 2 * width)
+    own = jnp.where(first, got[0], got[1])
+    other = jnp.where(first, got[1], got[0])
     block = jnp.concatenate([own, other], axis=2).reshape(Y * few, 4 * width)
     core = lax.axis_index("core").astype(jnp.int32).reshape(1)
     weights = [lax.all_gather(w, "core", axis=0) for w in (w_gate.T, w_up.T, w_down)]

time: 120 us -> 118 us (0.983)
  starting transfers between devices: 20.1 us -> 26.4 us
  blocking collectives: 85.8 us -> 80.5 us
  waiting for transfers between devices: 4.22 us -> 1.75 us
    all_to_all x1, starting transfers between devices: 4.03 us -> 10.1 us  [on_device(): terms = lax.all_to_all(term.reshape(X * Y, few, 2 * width), ROW, 0, 0)]
    all_to_all x2, blocking collectives: 38.9 us -> 35.7 us  [gather(): lax.all_to_all(jnp.broadcast_to(block[None], (count,) + block.shape), axi...]
    all_to_all x1, waiting for transfers between devices: 4.22 us -> 1.74 us  [on_device(): lax.all_to_all(sent, ('core', 'y'), 0, 0).reshape(2, Y, few, 2 * width)]
    all_to_all x1, blocking collectives: 28.8 us -> 26.6 us  [on_device(): lax.all_to_all(sent, 'z', 0, 0).astype(jnp.float32)]
where the time goes in v5:
time: 118 us; the launch traced here: 117 us
  blocking collectives  80.5 us (68%)
  starting transfers between devices  26.4 us (22%)
  Pallas kernels  5.01 us (4%)
  other arithmetic  1.82 us (2%)
  waiting for transfers between devices  1.75 us (1%)
    all_to_all x2, blocking collectives, gather(): lax.all_to_all(jnp.broadcast_to(block[None], (count,) + block.shape), axi...  35.7 us
    all_to_all x1, blocking collectives, on_device(): lax.all_to_all(sent, 'z', 0, 0).astype(jnp.float32)  26.6 us
    all_to_all x1, starting transfers between devices, on_device(): lax.all_to_all(sent, ('core', 'y'), 0, 0).reshape(2, Y, few, 2 * width)  10.2 us
    all_to_all x1, starting transfers between devices, on_device(): terms = lax.all_to_all(term.reshape(X * Y, few, 2 * width), ROW, 0, 0)  10.1 us
    all_gather x3, blocking collectives, on_device(): lax.all_gather(w, 'core', axis=0)  7.63 us
    all_gather x1, blocking collectives, on_device(): pairs = lax.all_gather(total, 'core', axis=0)  6.22 us
    ppermute x1, starting transfers between devices, on_device(): lax.ppermute(own, 'core', SWAP)  6.09 us
    pallas_call x1, Pallas kernels, backward(): pl.pallas_call(backward_kernel, grid_spec=pltpu.PrefetchScalarGridSpec(nu...  2.61 us
  transfers between devices with their start and end apart: 3, of which 1 were waited for; matrix products, arithmetic and copies ran while one was open for 0% of the time, Pallas kernels for 2%

profile of v5, /device:TPU:1, one launch (start us, length us, event | category | flops | bytes accessed | tf_op | source)
XLA Modules:
  0.0 117.3 jit_solution(12356348201167013660)
XLA Ops:
  0.6 0.0 copy-start.3
  0.6 0.8 maximum_bitcast_fusion.1
  1.4 0.7 broadcast_in_dim.9
  2.2 10.2 %all-to-all-start = ((bf16[16,8,1024]{2,1,0:T(8,128)(2,1)}), bf16[16,8,1024]{2,1,0:T(8,128)(2,1)S(1)}, u32[]{:S(2)}, u32[]{:S(2)}) async-start(bf16[16,8,1024]{2,1,0:T(8,128)(2,1)} %bitcast.2), calls=%async_computation | async-start | bytes 524288 | tf_op jit(solution)/shard_map/all_to_all | solution.py:145
  12.4 0.0 copy-done.3
  12.4 2.5 %all-gather = bf16[896,512]{1,0:T(8,128)(2,1)S(1)} all-gather(bf16[448,512]{1,0:T(8,128)(2,1)S(1)} %bitcast.38), channel_id=2, replica_groups=mesh['x'=4,'y'=8,'z'=8,'core'=2] {'core'}, dimensions={0}, use_global_device_ids=true | all-gather | bytes 1376256 | tf_op jit(solution)/shard_map/all_gather | solution.py:150
  14.9 0.0 copy-done.4
  14.9 2.6 %all-gather.1 = bf16[896,512]{1,0:T(8,128)(2,1)S(1)} all-gather(bf16[448,512]{1,0:T(8,128)(2,1)S(1)} %bitcast.39), channel_id=3, replica_groups=mesh['x'=4,'y'=8,'z'=8,'core'=2] {'core'}, dimensions={0}, use_global_device_ids=true | all-gather | bytes 1376256 | tf_op jit(solution)/shard_map/all_gather | solution.py:150
  17.5 0.0 copy-done.5
  17.5 2.6 %all-gather.2 = bf16[896,512]{1,0:T(8,128)(2,1)} all-gather(bf16[448,512]{1,0:T(8,128)(2,1)S(1)} %copy-done.5), channel_id=4, replica_groups=mesh['x'=4,'y'=8,'z'=8,'core'=2] {'core'}, dimensions={0}, use_global_device_ids=true | all-gather | bytes 1376256 | tf_op jit(solution)/shard_map/all_gather | solution.py:150
  20.1 1.7 %all-to-all-done = bf16[16,8,1024]{2,1,0:T(8,128)(2,1)S(1)} async-done(((bf16[16,8,1024]{2,1,0:T(8,128)(2,1)}), bf16[16,8,1024]{2,1,0:T(8,128)(2,1)S(1)}, u32[]{:S(2)}, u32[]{:S(2)}) %all-to-all-start) | async-done | bytes 262176 | tf_op jit(solution)/shard_map/all_to_all | solution.py:145
  21.9 0.1 broadcast_in_dim.10
  22.0 0.0 copy-start.2
  22.0 16.5 %all_to_all.25 = bf16[4,64,2048]{2,1,0:T(8,128)(2,1)S(1)} all-to-all(bf16[4,64,2048]{2,1,0:T(8,128)(2,1)S(1)} %broadcast_in_dim.10), channel_id=1, replica_groups=mesh['x'=4,'y'=8,'z'=8,'core'=2] {'x'}, dimensions={0} | all-to-all | bytes 2097152 | tf_op jit(solution)/shard_map/all_to_all | solution.py:17
  38.5 0.0 copy-done.2
  38.5 0.9 forward.1
  39.4 26.6 %all_to_all.26 = bf16[8,3,56,256]{3,2,1,0:T(8,128)(2,1)S(1)} all-to-all(bf16[8,3,56,256]{3,2,1,0:T(8,128)(2,1)S(1)} %forward.1), channel_id=1, replica_groups=mesh['x'=4,'y'=8,'z'=8,'core'=2] {'z'}, dimensions={0} | all-to-all | bytes 1376256 | tf_op jit(solution)/shard_map/all_to_all | solution.py:155
  66.0 0.1 convert_reduce_fusion
  66.2 19.2 %all_to_all.27 = bf16[8,3,56,256]{3,2,1,0:T(8,128)(2,1)S(1)} all-to-all(bf16[8,3,56,256]{3,2,1,0:T(8,128)(2,1)S(1)} %broadcast_in_dim.22), channel_id=1, replica_groups=mesh['x'=4,'y'=8,'z'=8,'core'=2] {'z'}, dimensions={0} | all-to-all | bytes 1376256 | tf_op jit(solution)/shard_map/all_to_all | solution.py:17
  85.5 0.0 copy-start
  85.5 1.5 %input_terms.1 = bf16[256,1024]{1,0:T(8,128)(2,1)} custom-call(s32[1]{0:T(128)} %bitcast.core_ref, bf16[3,448,256]{2,1,0:T(8,128)(2,1)S(1)} %bitcast.31, bf16[2,448,512]{2,1,0:T(8,128)(2,1)S(1)} %bitcast.28, bf16[2,448,512]{2,1,0:T(8,128)(2,1)S(1)} %bitcast.30), custom_call_target="tpu_custom_call" | custom-call | flops 469762048 | bytes 1835008 | tf_op jit(solution)/shard_map/input_terms/pallas_call | solution.py:120
  87.0 10.1 %all-to-all-start.4 = ((bf16[32,8,1024]{2,1,0:T(8,128)(2,1)}), bf16[32,8,1024]{2,1,0:T(8,128)(2,1)S(1)}, u32[]{:S(2)}, u32[]{:S(2)}) async-start(bf16[32,8,1024]{2,1,0:T(8,128)(2,1)} %bitcast.12), calls=%async_computation.4 | async-start | bytes 1048576 | tf_op jit(solution)/shard_map/all_to_all | solution.py:160
  97.1 6.1 %collective-permute-start = (bf16[3,448,256]{2,1,0:T(8,128)(2,1)S(1)}, bf16[3,448,256]{2,1,0:T(8,128)(2,1)S(1)}, u32[]{:S(2)}, u32[]{:S(2)}) collective-permute-start(bf16[3,448,256]{2,1,0:T(8,128)(2,1)S(1)} %bitcast.32), channel_id=1, source_target_pairs={{0,1},{1,0},{2,3},{3,2},{4,5},{5,4},{6,7},{7,6},{8,9},{9,8},{10,11... | collective-permute-start | bytes 2064392 | tf_op jit(solution)/shard_map/ppermute | solution.py:178
  103.3 2.2 %all-gather.5 = bf16[512,512]{1,0:T(8,128)(2,1)S(1)} all-gather(bf16[256,512]{1,0:T(8,128)(2,1)S(1)} %get-tuple-element.19), channel_id=7, replica_groups=mesh['x'=4,'y'=8,'z'=8,'core'=2] {'core'}, dimensions={0}, use_global_device_ids=true | all-gather | bytes 786432 | tf_op jit(solution)/shard_map/all_gather | solution.py:174
  105.4 2.2 %all-gather.4 = bf16[512,512]{1,0:T(8,128)(2,1)S(1)} all-gather(bf16[256,512]{1,0:T(8,128)(2,1)S(1)} %get-tuple-element.18), channel_id=6, replica_groups=mesh['x'=4,'y'=8,'z'=8,'core'=2] {'core'}, dimensions={0}, use_global_device_ids=true | all-gather | bytes 786432 | tf_op jit(solution)/shard_map/all_gather | solution.py:173
  107.6 0.1 pad_maximum_fusion.there_ref
  107.7 0.0 collective-permute-done.other_ref
  107.8 2.6 %backward.1 = (bf16[448,512]{1,0:T(8,128)(2,1)}, bf16[448,512]{1,0:T(8,128)(2,1)}, bf16[448,512]{1,0:T(8,128)(2,1)}) custom-call(s32[1]{0:T(128)} %bitcast.core_ref, bf16[3,448,256]{2,1,0:T(8,128)(2,1)S(1)} %bitcast.33, bf16[3,448,256]{2,1,0:T(8,128)(2,1)S(1)} %collective-permute-done.other_ref, bf16[256,2048]{1,0:T(8,128)(2,1)S(1)} %bitcast.26, ...), custom_call_target="tpu_custom_call" | custom-call | flops 704643072 | bytes 1835008 | tf_op jit(solution)/shard_map/backward/pallas_call | solution.py:85
  110.4 0.0 all-to-all-done.4
  110.4 0.1 reduce_sum.22
  110.5 6.2 %all-gather.3 = bf16[16,1024]{1,0:T(8,128)(2,1)S(1)} all-gather(bf16[8,1024]{1,0:T(8,128)(2,1)S(1)} %reduce_sum.22), channel_id=5, replica_groups=mesh['x'=4,'y'=8,'z'=8,'core'=2] {'core'}, dimensions={0}, use_global_device_ids=true | all-gather | bytes 49152 | tf_op jit(solution)/shard_map/all_gather | solution.py:162
  116.7 0.6 pad_maximum_fusion.2
  (13 shorter events, 0.2 us)
Async XLA Ops:
  0.6 11.8 %copy-start.3 = (bf16[512,448]{0,1:T(8,128)(2,1)S(1)}, bf16[512,448]{0,1:T(8,128)(2,1)}, u32[]{:S(2)}) copy-start(bf16[512,448]{0,1:T(8,128)(2,1)} %param.7) | copy-start | bytes 1376260
  1.4 13.5 %copy-start.4 = (bf16[512,448]{0,1:T(8,128)(2,1)S(1)}, bf16[512,448]{0,1:T(8,128)(2,1)}, u32[]{:S(2)}) copy-start(bf16[512,448]{0,1:T(8,128)(2,1)} %param.8) | copy-start | bytes 1376260
  2.2 19.6 %all-to-all-start = ((bf16[16,8,1024]{2,1,0:T(8,128)(2,1)}), bf16[16,8,1024]{2,1,0:T(8,128)(2,1)S(1)}, u32[]{:S(2)}, u32[]{:S(2)}) async-start(bf16[16,8,1024]{2,1,0:T(8,128)(2,1)} %bitcast.2), calls=%async_computation | async-start | bytes 524288 | tf_op jit(solution)/shard_map/all_to_all | solution.py:145
  14.9 2.6 %copy-start.5 = (bf16[448,512]{1,0:T(8,128)(2,1)S(1)}, bf16[448,512]{1,0:T(8,128)(2,1)}, u32[]{:S(2)}) copy-start(bf16[448,512]{1,0:T(8,128)(2,1)} %param.9) | copy-start | bytes 1376260
  22.0 16.5 %copy-start.2 = (bf16[896,512]{1,0:T(8,128)(2,1)S(1)}, bf16[896,512]{1,0:T(8,128)(2,1)}, u32[]{:S(2)}) copy-start(bf16[896,512]{1,0:T(8,128)(2,1)} %all-gather.2) | copy-start | bytes 2752516
  85.5 1.5 %copy-start = (bf16[3,8,56,256]{3,2,1,0:T(8,128)(2,1)}, bf16[3,8,56,256]{3,2,1,0:T(8,128)(2,1)S(1)}, u32[]{:S(2)}) copy-start(bf16[3,8,56,256]{3,2,1,0:T(8,128)(2,1)S(1)} %copy.9) | copy-start | bytes 2064388
  87.0 10.1 %copy-start.1 = (bf16[3,8,56,256]{3,2,1,0:T(8,128)(2,1)S(1)}, bf16[3,8,56,256]{3,2,1,0:T(8,128)(2,1)}, u32[]{:S(2)}) copy-start(bf16[3,8,56,256]{3,2,1,0:T(8,128)(2,1)} %copy-done) | copy-start | bytes 2064388
  87.0 23.3 %all-to-all-start.4 = ((bf16[32,8,1024]{2,1,0:T(8,128)(2,1)}), bf16[32,8,1024]{2,1,0:T(8,128)(2,1)S(1)}, u32[]{:S(2)}, u32[]{:S(2)}) async-start(bf16[32,8,1024]{2,1,0:T(8,128)(2,1)} %bitcast.12), calls=%async_computation.4 | async-start | bytes 1048576 | tf_op jit(solution)/shard_map/all_to_all | solution.py:160
  97.1 10.6 %collective-permute-start = (bf16[3,448,256]{2,1,0:T(8,128)(2,1)S(1)}, bf16[3,448,256]{2,1,0:T(8,128)(2,1)S(1)}, u32[]{:S(2)}, u32[]{:S(2)}) collective-permute-start(bf16[3,448,256]{2,1,0:T(8,128)(2,1)S(1)} %bitcast.32), channel_id=1, source_target_pairs={{0,1},{1,0},{2,3},{3,2},{4,5},{5,4},{6,7},{7,6},{8,9},{9,8},{10,11... | collective-permute-start | bytes 2064392 | tf_op jit(solution)/shard_map/ppermute | solution.py:178

commit v6 on v5

--- a/solution.py
+++ b/solution.py
@@ -7,8 +7,10 @@
 from jax.sharding import PartitionSpec as P
 
 X, Y, Z = 4, 8, 8
-ROW = ("x", "y")
-COL = ("z", "core")
+ROW = ("x", "y_high", "y_low")
+COL = ("z_high", "z_low", "core")
+Y_PEERS = ("y_low", "y_high")
+Z_PEERS = ("z_low", "z_high")
 SWAP = ((0, 1), (1, 0))
 PARAMS = pltpu.CompilerParams(vmem_limit_bytes=16 * 1024 * 1024)
 
@@ -142,7 +144,7 @@
 
     sent = jnp.concatenate([activations, out_grad], axis=1).reshape(2, 1, few, 2 * width)
     sent = jnp.broadcast_to(sent, (2, Y, few, 2 * width)).reshape(2 * Y, few, 2 * width)
-    got = lax.all_to_all(sent, ("core", "y"), 0, 0).reshape(2, Y, few, 2 * width)
+    got = lax.all_to_all(sent, ("core",) + Y_PEERS, 0, 0).reshape(2, Y, few, 2 * width)
     own = jnp.where(first, got[0], got[1])
     other = jnp.where(first, got[1], got[0])
     block = jnp.concatenate([own, other], axis=2).reshape(Y * few, 4 * width)
@@ -152,12 +154,12 @@
     both = gather(block, "x", X).reshape(half, 4 * width)
 
     sent = forward(core, weights, both)
-    summed = jnp.sum(lax.all_to_all(sent, "z", 0, 0).astype(jnp.float32), axis=0)
+    summed = jnp.sum(lax.all_to_all(sent, Z_PEERS, 0, 0).astype(jnp.float32), axis=0)
     mine = swiglu_parts(summed[0], summed[1], summed[2])
-    own = gather(mine, "z", Z).transpose(1, 0, 2, 3).reshape(3, units, half)
+    own = gather(mine, Z_PEERS, Z).transpose(1, 0, 2, 3).reshape(3, units, half)
 
     term = input_terms(core, own, weights)
-    terms = lax.all_to_all(term.reshape(X * Y, few, 2 * width), ROW, 0, 0)
+    terms = lax.all_to_all(term.reshape(X * Y, few, 2 * width), ("x",) + Y_PEERS, 0, 0)
     total = jnp.sum(terms.astype(jnp.float32), axis=0).astype(jnp.bfloat16)
     pairs = lax.all_gather(total, "core", axis=0)
     in_grad = jnp.concatenate(
@@ -182,7 +184,7 @@
 
 
 def solution(mesh):
-    grid = Mesh(mesh.devices.reshape(X, Y, Z, 2), ROW + COL)
+    grid = Mesh(mesh.devices.reshape(X, 2, Y // 2, 2, Z // 2, 2), ROW + COL)
     return jax.shard_map(
         on_device,
         mesh=grid,

time: 118 us -> 116 us (0.983)
  blocking collectives: 80.5 us -> 78.7 us
  starting transfers between devices: 26.4 us -> 24.8 us
    all_to_all x1, blocking collectives: 26.6 us -> 23.3 us  [on_device(): lax.all_to_all(sent, Z_PEERS, 0, 0).astype(jnp.float32)]
    all_to_all x2, starting transfers between devices: 20.3 us -> 18.6 us  [the longest x1 10.2 us: on_device(): lax.all_to_all(sent, ('core',) + Y_PEERS, 0, 0)]
where the time goes in v6:
time: 116 us; the launch traced here: 115 us
  blocking collectives  78.7 us (68%)
  starting transfers between devices  24.8 us (21%)
  Pallas kernels  5.01 us (4%)
  waiting for transfers between devices  2.78 us (2%)
  other arithmetic  1.82 us (2%)
    all_to_all x2, blocking collectives, gather(): lax.all_to_all(jnp.broadcast_to(block[None], (count,) + block.shape), axi...  36.4 us
    all_to_all x1, blocking collectives, on_device(): lax.all_to_all(sent, Z_PEERS, 0, 0).astype(jnp.float32)  23.3 us
    all_to_all x1, starting transfers between devices, on_device(): lax.all_to_all(sent, ('core',) + Y_PEERS, 0, 0)  10.2 us
    all_to_all x1, starting transfers between devices, on_device(): lax.all_to_all(term.reshape(X * Y, few, 2 * width), ('x',) + Y_PEERS, 0, 0)  8.37 us
    all_gather x3, blocking collectives, on_device(): lax.all_gather(w, 'core', axis=0)  7.63 us
    all_gather x1, blocking collectives, on_device(): pairs = lax.all_gather(total, 'core', axis=0)  6.98 us
    ppermute x1, starting transfers between devices, on_device(): lax.ppermute(own, 'core', SWAP)  6.22 us
    all_to_all x1, waiting for transfers between devices, on_device(): lax.all_to_all(sent, ('core',) + Y_PEERS, 0, 0)  2.78 us
  transfers between devices with their start and end apart: 3, of which 1 were waited for; matrix products, arithmetic and copies ran while one was open for 0% of the time, Pallas kernels for 2%

profile of v6, /device:TPU:1, one launch (start us, length us, event | category | flops | bytes accessed | tf_op | source)
XLA Modules:
  0.0 114.9 jit_solution(13401189632619806182)
XLA Ops:
  0.6 0.0 copy-start.3
  0.6 0.8 maximum_bitcast_fusion.1
  1.4 0.7 broadcast_in_dim.9
  2.2 10.2 %all-to-all-start = ((bf16[16,8,1024]{2,1,0:T(8,128)(2,1)}), bf16[16,8,1024]{2,1,0:T(8,128)(2,1)S(1)}, u32[]{:S(2)}, u32[]{:S(2)}) async-start(bf16[16,8,1024]{2,1,0:T(8,128)(2,1)} %bitcast.2), calls=%async_computation | async-start | bytes 524288 | tf_op jit(solution)/shard_map/all_to_all | solution.py:147
  12.4 0.0 copy-done.3
  12.4 2.5 %all-gather = bf16[896,512]{1,0:T(8,128)(2,1)S(1)} all-gather(bf16[448,512]{1,0:T(8,128)(2,1)S(1)} %bitcast.38), channel_id=2, replica_groups=mesh['x'=4,'y_high'=2,'y_low'=4,'z_high'=2,'z_low'=4,'core'=2] {'core'}, dimensions={0}, use_global_device_ids=true | all-gather | bytes 1376256 | tf_op jit(solution)/shard_map/all_gather | solution.py:152
  14.9 0.0 copy-done.4
  14.9 2.6 %all-gather.1 = bf16[896,512]{1,0:T(8,128)(2,1)S(1)} all-gather(bf16[448,512]{1,0:T(8,128)(2,1)S(1)} %bitcast.39), channel_id=3, replica_groups=mesh['x'=4,'y_high'=2,'y_low'=4,'z_high'=2,'z_low'=4,'core'=2] {'core'}, dimensions={0}, use_global_device_ids=true | all-gather | bytes 1376256 | tf_op jit(solution)/shard_map/all_gather | solution.py:152
  17.5 0.0 copy-done.5
  17.5 2.6 %all-gather.2 = bf16[896,512]{1,0:T(8,128)(2,1)} all-gather(bf16[448,512]{1,0:T(8,128)(2,1)S(1)} %copy-done.5), channel_id=4, replica_groups=mesh['x'=4,'y_high'=2,'y_low'=4,'z_high'=2,'z_low'=4,'core'=2] {'core'}, dimensions={0}, use_global_device_ids=true | all-gather | bytes 1376256 | tf_op jit(solution)/shard_map/all_gather | solution.py:152
  20.1 2.8 %all-to-all-done = bf16[16,8,1024]{2,1,0:T(8,128)(2,1)S(1)} async-done(((bf16[16,8,1024]{2,1,0:T(8,128)(2,1)}), bf16[16,8,1024]{2,1,0:T(8,128)(2,1)S(1)}, u32[]{:S(2)}, u32[]{:S(2)}) %all-to-all-start) | async-done | bytes 262176 | tf_op jit(solution)/shard_map/all_to_all | solution.py:147
  22.9 0.1 broadcast_in_dim.10
  23.0 0.0 copy-start.2
  23.0 16.0 %all_to_all.25 = bf16[4,64,2048]{2,1,0:T(8,128)(2,1)S(1)} all-to-all(bf16[4,64,2048]{2,1,0:T(8,128)(2,1)S(1)} %broadcast_in_dim.10), channel_id=1, replica_groups=mesh['x'=4,'y_high'=2,'y_low'=4,'z_high'=2,'z_low'=4,'core'=2] {'x'}, dimensions={0} | all-to-all | bytes 2097152 | tf_op jit(solution)/shard_map/all_to_all | solution.py:19
  39.0 0.0 copy-done.2
  39.0 0.9 forward.1
  39.9 23.3 %all_to_all.26 = bf16[8,3,56,256]{3,2,1,0:T(8,128)(2,1)S(1)} all-to-all(bf16[8,3,56,256]{3,2,1,0:T(8,128)(2,1)S(1)} %forward.1), channel_id=1, replica_groups=mesh['x'=4,'y_high'=2,'y_low'=4,'z_high'=2,'z_low'=4,'core'=2] {'z_low',..., dimensions={0} | all-to-all | bytes 1376256 | tf_op jit(solution)/shard_map/all_to_all | solution.py:157
  63.2 0.1 convert_reduce_fusion
  63.5 20.4 %all_to_all.27 = bf16[8,3,56,256]{3,2,1,0:T(8,128)(2,1)S(1)} all-to-all(bf16[8,3,56,256]{3,2,1,0:T(8,128)(2,1)S(1)} %broadcast_in_dim.22), channel_id=1, replica_groups=mesh['x'=4,'y_high'=2,'y_low'=4,'z_high'=2,'z_low'=4,'core'=2] {'z_low',..., dimensions={0} | all-to-all | bytes 1376256 | tf_op jit(solution)/shard_map/all_to_all | solution.py:19
  83.9 0.0 copy-start
  83.9 1.5 %input_terms.1 = bf16[256,1024]{1,0:T(8,128)(2,1)} custom-call(s32[1]{0:T(128)} %bitcast.core_ref, bf16[3,448,256]{2,1,0:T(8,128)(2,1)S(1)} %bitcast.31, bf16[2,448,512]{2,1,0:T(8,128)(2,1)S(1)} %bitcast.28, bf16[2,448,512]{2,1,0:T(8,128)(2,1)S(1)} %bitcast.30), custom_call_target="tpu_custom_call" | custom-call | flops 469762048 | bytes 1835008 | tf_op jit(solution)/shard_map/input_terms/pallas_call | solution.py:122
  85.4 8.4 %all-to-all-start.4 = ((bf16[32,8,1024]{2,1,0:T(8,128)(2,1)}), bf16[32,8,1024]{2,1,0:T(8,128)(2,1)S(1)}, u32[]{:S(2)}, u32[]{:S(2)}) async-start(bf16[32,8,1024]{2,1,0:T(8,128)(2,1)} %bitcast.12), calls=%async_computation.4 | async-start | bytes 1048576 | tf_op jit(solution)/shard_map/all_to_all | solution.py:162
  93.8 6.2 %collective-permute-start = (bf16[3,448,256]{2,1,0:T(8,128)(2,1)S(1)}, bf16[3,448,256]{2,1,0:T(8,128)(2,1)S(1)}, u32[]{:S(2)}, u32[]{:S(2)}) collective-permute-start(bf16[3,448,256]{2,1,0:T(8,128)(2,1)S(1)} %bitcast.32), channel_id=1, source_target_pairs={{0,1},{1,0},{2,3},{3,2},{4,5},{5,4},{6,7},{7,6},{8,9},{9,8},{10,11... | collective-permute-start | bytes 2064392 | tf_op jit(solution)/shard_map/ppermute | solution.py:180
  100.1 2.2 %all-gather.5 = bf16[512,512]{1,0:T(8,128)(2,1)S(1)} all-gather(bf16[256,512]{1,0:T(8,128)(2,1)S(1)} %get-tuple-element.19), channel_id=7, replica_groups=mesh['x'=4,'y_high'=2,'y_low'=4,'z_high'=2,'z_low'=4,'core'=2] {'core'}, dimensions={0}, use_global_device_ids=true | all-gather | bytes 786432 | tf_op jit(solution)/shard_map/all_gather | solution.py:176
  102.3 2.2 %all-gather.4 = bf16[512,512]{1,0:T(8,128)(2,1)S(1)} all-gather(bf16[256,512]{1,0:T(8,128)(2,1)S(1)} %get-tuple-element.18), channel_id=6, replica_groups=mesh['x'=4,'y_high'=2,'y_low'=4,'z_high'=2,'z_low'=4,'core'=2] {'core'}, dimensions={0}, use_global_device_ids=true | all-gather | bytes 786432 | tf_op jit(solution)/shard_map/all_gather | solution.py:175
  104.4 0.1 pad_maximum_fusion.there_ref
  104.6 0.0 collective-permute-done.other_ref
  104.6 2.6 %backward.1 = (bf16[448,512]{1,0:T(8,128)(2,1)}, bf16[448,512]{1,0:T(8,128)(2,1)}, bf16[448,512]{1,0:T(8,128)(2,1)}) custom-call(s32[1]{0:T(128)} %bitcast.core_ref, bf16[3,448,256]{2,1,0:T(8,128)(2,1)S(1)} %bitcast.33, bf16[3,448,256]{2,1,0:T(8,128)(2,1)S(1)} %collective-permute-done.other_ref, bf16[256,2048]{1,0:T(8,128)(2,1)S(1)} %bitcast.26, ...), custom_call_target="tpu_custom_call" | custom-call | flops 704643072 | bytes 1835008 | tf_op jit(solution)/shard_map/backward/pallas_call | solution.py:87
  107.2 0.0 all-to-all-done.4
  107.2 0.1 reduce_sum.22
  107.3 7.0 %all-gather.3 = bf16[16,1024]{1,0:T(8,128)(2,1)S(1)} all-gather(bf16[8,1024]{1,0:T(8,128)(2,1)S(1)} %reduce_sum.22), channel_id=5, replica_groups=mesh['x'=4,'y_high'=2,'y_low'=4,'z_high'=2,'z_low'=4,'core'=2] {'core'}, dimensions={0}, use_global_device_ids=true | all-gather | bytes 49152 | tf_op jit(solution)/shard_map/all_gather | solution.py:164
  114.3 0.6 pad_maximum_fusion.2
  (13 shorter events, 0.2 us)
Async XLA Ops:
  0.6 11.8 %copy-start.3 = (bf16[512,448]{0,1:T(8,128)(2,1)S(1)}, bf16[512,448]{0,1:T(8,128)(2,1)}, u32[]{:S(2)}) copy-start(bf16[512,448]{0,1:T(8,128)(2,1)} %param.7) | copy-start | bytes 1376260
  1.4 13.5 %copy-start.4 = (bf16[512,448]{0,1:T(8,128)(2,1)S(1)}, bf16[512,448]{0,1:T(8,128)(2,1)}, u32[]{:S(2)}) copy-start(bf16[512,448]{0,1:T(8,128)(2,1)} %param.8) | copy-start | bytes 1376260
  2.2 20.7 %all-to-all-start = ((bf16[16,8,1024]{2,1,0:T(8,128)(2,1)}), bf16[16,8,1024]{2,1,0:T(8,128)(2,1)S(1)}, u32[]{:S(2)}, u32[]{:S(2)}) async-start(bf16[16,8,1024]{2,1,0:T(8,128)(2,1)} %bitcast.2), calls=%async_computation | async-start | bytes 524288 | tf_op jit(solution)/shard_map/all_to_all | solution.py:147
  14.9 2.6 %copy-start.5 = (bf16[448,512]{1,0:T(8,128)(2,1)S(1)}, bf16[448,512]{1,0:T(8,128)(2,1)}, u32[]{:S(2)}) copy-start(bf16[448,512]{1,0:T(8,128)(2,1)} %param.9) | copy-start | bytes 1376260
  23.0 16.0 %copy-start.2 = (bf16[896,512]{1,0:T(8,128)(2,1)S(1)}, bf16[896,512]{1,0:T(8,128)(2,1)}, u32[]{:S(2)}) copy-start(bf16[896,512]{1,0:T(8,128)(2,1)} %all-gather.2) | copy-start | bytes 2752516
  83.9 1.5 %copy-start = (bf16[3,8,56,256]{3,2,1,0:T(8,128)(2,1)}, bf16[3,8,56,256]{3,2,1,0:T(8,128)(2,1)S(1)}, u32[]{:S(2)}) copy-start(bf16[3,8,56,256]{3,2,1,0:T(8,128)(2,1)S(1)} %copy.9) | copy-start | bytes 2064388
  85.4 8.4 %copy-start.1 = (bf16[3,8,56,256]{3,2,1,0:T(8,128)(2,1)S(1)}, bf16[3,8,56,256]{3,2,1,0:T(8,128)(2,1)}, u32[]{:S(2)}) copy-start(bf16[3,8,56,256]{3,2,1,0:T(8,128)(2,1)} %copy-done) | copy-start | bytes 2064388
  85.4 21.8 %all-to-all-start.4 = ((bf16[32,8,1024]{2,1,0:T(8,128)(2,1)}), bf16[32,8,1024]{2,1,0:T(8,128)(2,1)S(1)}, u32[]{:S(2)}, u32[]{:S(2)}) async-start(bf16[32,8,1024]{2,1,0:T(8,128)(2,1)} %bitcast.12), calls=%async_computation.4 | async-start | bytes 1048576 | tf_op jit(solution)/shard_map/all_to_all | solution.py:162
  93.8 10.8 %collective-permute-start = (bf16[3,448,256]{2,1,0:T(8,128)(2,1)S(1)}, bf16[3,448,256]{2,1,0:T(8,128)(2,1)S(1)}, u32[]{:S(2)}, u32[]{:S(2)}) collective-permute-start(bf16[3,448,256]{2,1,0:T(8,128)(2,1)S(1)} %bitcast.32), channel_id=1, source_target_pairs={{0,1},{1,0},{2,3},{3,2},{4,5},{5,4},{6,7},{7,6},{8,9},{9,8},{10,11... | collective-permute-start | bytes 2064392 | tf_op jit(solution)/shard_map/ppermute | solution.py:180

commit v7 on v6

--- a/solution.py
+++ b/solution.py
@@ -7,10 +7,11 @@
 from jax.sharding import PartitionSpec as P
 
 X, Y, Z = 4, 8, 8
-ROW = ("x", "y_high", "y_low")
-COL = ("z_high", "z_low", "core")
-Y_PEERS = ("y_low", "y_high")
-Z_PEERS = ("z_low", "z_high")
+ROW = ("x1", "x0", "y2", "y1", "y0")
+COL = ("z2", "z1", "z0", "core")
+X_PEERS = ("x1", "x0")
+Y_PEERS = ("y1", "y0", "y2")
+Z_PEERS = ("z1", "z2", "z0")
 SWAP = ((0, 1), (1, 0))
 PARAMS = pltpu.CompilerParams(vmem_limit_bytes=16 * 1024 * 1024)
 
@@ -151,7 +152,7 @@
     core = lax.axis_index("core").astype(jnp.int32).reshape(1)
     weights = [lax.all_gather(w, "core", axis=0) for w in (w_gate.T, w_up.T, w_down)]
     block, weights = lax.optimization_barrier((block, weights))
-    both = gather(block, "x", X).reshape(half, 4 * width)
+    both = gather(block, X_PEERS, X).reshape(half, 4 * width)
 
     sent = forward(core, weights, both)
     summed = jnp.sum(lax.all_to_all(sent, Z_PEERS, 0, 0).astype(jnp.float32), axis=0)
@@ -159,7 +160,7 @@
     own = gather(mine, Z_PEERS, Z).transpose(1, 0, 2, 3).reshape(3, units, half)
 
     term = input_terms(core, own, weights)
-    terms = lax.all_to_all(term.reshape(X * Y, few, 2 * width), ("x",) + Y_PEERS, 0, 0)
+    terms = lax.all_to_all(term.reshape(X * Y, few, 2 * width), X_PEERS + Y_PEERS, 0, 0)
     total = jnp.sum(terms.astype(jnp.float32), axis=0).astype(jnp.bfloat16)
     pairs = lax.all_gather(total, "core", axis=0)
     in_grad = jnp.concatenate(
@@ -184,7 +185,7 @@
 
 
 def solution(mesh):
-    grid = Mesh(mesh.devices.reshape(X, 2, Y // 2, 2, Z // 2, 2), ROW + COL)
+    grid = Mesh(mesh.devices.reshape((2,) * 9), ROW + COL)
     return jax.shard_map(
         on_device,
         mesh=grid,

time: 116 us -> 115 us (level)
    all_to_all x1, blocking collectives: 23.3 us -> 25 us  [on_device(): lax.all_to_all(sent, Z_PEERS, 0, 0).astype(jnp.float32)]
    all_to_all x2, blocking collectives: 36.4 us -> 35 us  [gather(): lax.all_to_all(jnp.broadcast_to(block[None], (count,) + block.shape), axi...]
    ppermute x1, starting transfers between devices: 6.22 us -> 7.45 us  [on_device(): lax.ppermute(own, 'core', SWAP)]
where the time goes in v7:
time: 115 us
  blocking collectives  78.2 us (68%)
  starting transfers between devices  25.3 us (22%)
  Pallas kernels  5.02 us (4%)
  waiting for transfers between devices  2.78 us (2%)
  other arithmetic  1.82 us (2%)
    all_to_all x2, blocking collectives, gather(): lax.all_to_all(jnp.broadcast_to(block[None], (count,) + block.shape), axi...  35 us
    all_to_all x1, blocking collectives, on_device(): lax.all_to_all(sent, Z_PEERS, 0, 0).astype(jnp.float32)  25 us
    all_to_all x1, starting transfers between devices, on_device(): lax.all_to_all(sent, ('core',) + Y_PEERS, 0, 0)  10.2 us
    all_gather x3, blocking collectives, on_device(): lax.all_gather(w, 'core', axis=0)  7.63 us
    all_to_all x1, starting transfers between devices, on_device(): lax.all_to_all(term.reshape(X * Y, few, 2 * width), X_PEERS + Y_PEERS, 0, 0)  7.55 us
    ppermute x1, starting transfers between devices, on_device(): lax.ppermute(own, 'core', SWAP)  7.45 us
    all_gather x1, blocking collectives, on_device(): pairs = lax.all_gather(total, 'core', axis=0)  6.17 us
    all_to_all x1, waiting for transfers between devices, on_device(): lax.all_to_all(sent, ('core',) + Y_PEERS, 0, 0)  2.78 us
  transfers between devices with their start and end apart: 3, of which 1 were waited for; matrix products, arithmetic and copies ran while one was open for 0% of the time, Pallas kernels for 2%

profile of v7, /device:TPU:1, one launch (start us, length us, event | category | flops | bytes accessed | tf_op | source)
XLA Modules:
  0.0 114.8 jit_solution(3121151405056918421)
XLA Ops:
  0.6 0.0 copy-start.3
  0.6 0.8 maximum_bitcast_fusion.1
  1.4 0.7 broadcast_in_dim.9
  2.2 10.2 %all-to-all-start = ((bf16[16,8,1024]{2,1,0:T(8,128)(2,1)}), bf16[16,8,1024]{2,1,0:T(8,128)(2,1)S(1)}, u32[]{:S(2)}, u32[]{:S(2)}) async-start(bf16[16,8,1024]{2,1,0:T(8,128)(2,1)} %bitcast.2), calls=%async_computation | async-start | bytes 524288 | tf_op jit(solution)/shard_map/all_to_all | solution.py:148
  12.4 0.0 copy-done.3
  12.4 2.5 %all-gather = bf16[896,512]{1,0:T(8,128)(2,1)S(1)} all-gather(bf16[448,512]{1,0:T(8,128)(2,1)S(1)} %bitcast.38), channel_id=2, replica_groups=mesh['x1'=2,'x0'=2,'y2'=2,'y1'=2,'y0'=2,'z2'=2,'z1'=2,'z0'=2,'core'=2] {..., dimensions={0}, use_global_device_ids=true | all-gather | bytes 1376256 | tf_op jit(solution)/shard_map/all_gather | solution.py:153
  14.9 0.0 copy-done.4
  14.9 2.6 %all-gather.1 = bf16[896,512]{1,0:T(8,128)(2,1)S(1)} all-gather(bf16[448,512]{1,0:T(8,128)(2,1)S(1)} %bitcast.39), channel_id=3, replica_groups=mesh['x1'=2,'x0'=2,'y2'=2,'y1'=2,'y0'=2,'z2'=2,'z1'=2,'z0'=2,'core'=2] {..., dimensions={0}, use_global_device_ids=true | all-gather | bytes 1376256 | tf_op jit(solution)/shard_map/all_gather | solution.py:153
  17.5 0.0 copy-done.5
  17.5 2.6 %all-gather.2 = bf16[896,512]{1,0:T(8,128)(2,1)} all-gather(bf16[448,512]{1,0:T(8,128)(2,1)S(1)} %copy-done.5), channel_id=4, replica_groups=mesh['x1'=2,'x0'=2,'y2'=2,'y1'=2,'y0'=2,'z2'=2,'z1'=2,'z0'=2,'core'=2] {..., dimensions={0}, use_global_device_ids=true | all-gather | bytes 1376256 | tf_op jit(solution)/shard_map/all_gather | solution.py:153
  20.1 2.8 %all-to-all-done = bf16[16,8,1024]{2,1,0:T(8,128)(2,1)S(1)} async-done(((bf16[16,8,1024]{2,1,0:T(8,128)(2,1)}), bf16[16,8,1024]{2,1,0:T(8,128)(2,1)S(1)}, u32[]{:S(2)}, u32[]{:S(2)}) %all-to-all-start) | async-done | bytes 262176 | tf_op jit(solution)/shard_map/all_to_all | solution.py:148
  22.9 0.1 broadcast_in_dim.10
  23.0 0.0 copy-start.2
  23.0 16.0 %all_to_all.25 = bf16[4,64,2048]{2,1,0:T(8,128)(2,1)S(1)} all-to-all(bf16[4,64,2048]{2,1,0:T(8,128)(2,1)S(1)} %broadcast_in_dim.10), channel_id=1, replica_groups=mesh['x1'=2,'x0'=2,'y2'=2,'y1'=2,'y0'=2,'z2'=2,'z1'=2,'z0'=2,'core'=2] {..., dimensions={0} | all-to-all | bytes 2097152 | tf_op jit(solution)/shard_map/all_to_all | solution.py:20
  39.0 0.0 copy-done.2
  39.0 0.9 forward.1
  39.9 25.0 %all_to_all.26 = bf16[8,3,56,256]{3,2,1,0:T(8,128)(2,1)S(1)} all-to-all(bf16[8,3,56,256]{3,2,1,0:T(8,128)(2,1)S(1)} %forward.1), channel_id=1, replica_groups=mesh['x1'=2,'x0'=2,'y2'=2,'y1'=2,'y0'=2,'z2'=2,'z1'=2,'z0'=2,'core'=2] {..., dimensions={0} | all-to-all | bytes 1376256 | tf_op jit(solution)/shard_map/all_to_all | solution.py:158
  65.0 0.1 convert_reduce_fusion
  65.2 19.0 %all_to_all.27 = bf16[8,3,56,256]{3,2,1,0:T(8,128)(2,1)S(1)} all-to-all(bf16[8,3,56,256]{3,2,1,0:T(8,128)(2,1)S(1)} %broadcast_in_dim.22), channel_id=1, replica_groups=mesh['x1'=2,'x0'=2,'y2'=2,'y1'=2,'y0'=2,'z2'=2,'z1'=2,'z0'=2,'core'=2] {..., dimensions={0} | all-to-all | bytes 1376256 | tf_op jit(solution)/shard_map/all_to_all | solution.py:20
  84.3 1.5 %input_terms.1 = bf16[256,1024]{1,0:T(8,128)(2,1)} custom-call(s32[1]{0:T(128)} %bitcast.core_ref, bf16[3,448,256]{2,1,0:T(8,128)(2,1)S(1)} %bitcast.31, bf16[2,448,512]{2,1,0:T(8,128)(2,1)S(1)} %bitcast.28, bf16[2,448,512]{2,1,0:T(8,128)(2,1)S(1)} %bitcast.30), custom_call_target="tpu_custom_call" | custom-call | flops 469762048 | bytes 1835008 | tf_op jit(solution)/shard_map/input_terms/pallas_call | solution.py:123
  85.8 7.6 %all-to-all-start.4 = ((bf16[32,8,1024]{2,1,0:T(8,128)(2,1)}), bf16[32,8,1024]{2,1,0:T(8,128)(2,1)S(1)}, u32[]{:S(2)}, u32[]{:S(2)}) async-start(bf16[32,8,1024]{2,1,0:T(8,128)(2,1)} %bitcast.12), calls=%async_computation.4 | async-start | bytes 1048576 | tf_op jit(solution)/shard_map/all_to_all | solution.py:163
  93.3 0.0 copy-done.1
  93.3 7.5 %collective-permute-start = (bf16[3,448,256]{2,1,0:T(8,128)(2,1)S(1)}, bf16[3,448,256]{2,1,0:T(8,128)(2,1)S(1)}, u32[]{:S(2)}, u32[]{:S(2)}) collective-permute-start(bf16[3,448,256]{2,1,0:T(8,128)(2,1)S(1)} %bitcast.32), channel_id=1, source_target_pairs={{0,1},{1,0},{2,3},{3,2},{4,5},{5,4},{6,7},{7,6},{8,9},{9,8},{10,11... | collective-permute-start | bytes 2064392 | tf_op jit(solution)/shard_map/ppermute | solution.py:181
  100.8 2.2 %all-gather.5 = bf16[512,512]{1,0:T(8,128)(2,1)S(1)} all-gather(bf16[256,512]{1,0:T(8,128)(2,1)S(1)} %get-tuple-element.19), channel_id=7, replica_groups=mesh['x1'=2,'x0'=2,'y2'=2,'y1'=2,'y0'=2,'z2'=2,'z1'=2,'z0'=2,'core'=2] {..., dimensions={0}, use_global_device_ids=true | all-gather | bytes 786432 | tf_op jit(solution)/shard_map/all_gather | solution.py:177
  103.0 2.2 %all-gather.4 = bf16[512,512]{1,0:T(8,128)(2,1)S(1)} all-gather(bf16[256,512]{1,0:T(8,128)(2,1)S(1)} %get-tuple-element.18), channel_id=6, replica_groups=mesh['x1'=2,'x0'=2,'y2'=2,'y1'=2,'y0'=2,'z2'=2,'z1'=2,'z0'=2,'core'=2] {..., dimensions={0}, use_global_device_ids=true | all-gather | bytes 786432 | tf_op jit(solution)/shard_map/all_gather | solution.py:176
  105.2 0.1 pad_maximum_fusion.there_ref
  105.3 0.0 collective-permute-done.other_ref
  105.4 2.6 %backward.1 = (bf16[448,512]{1,0:T(8,128)(2,1)}, bf16[448,512]{1,0:T(8,128)(2,1)}, bf16[448,512]{1,0:T(8,128)(2,1)}) custom-call(s32[1]{0:T(128)} %bitcast.core_ref, bf16[3,448,256]{2,1,0:T(8,128)(2,1)S(1)} %bitcast.33, bf16[3,448,256]{2,1,0:T(8,128)(2,1)S(1)} %collective-permute-done.other_ref, bf16[256,2048]{1,0:T(8,128)(2,1)S(1)} %bitcast.26, ...), custom_call_target="tpu_custom_call" | custom-call | flops 704643072 | bytes 1835008 | tf_op jit(solution)/shard_map/backward/pallas_call | solution.py:88
  108.0 0.0 all-to-all-done.4
  108.0 0.1 reduce_sum.22
  108.1 6.2 %all-gather.3 = bf16[16,1024]{1,0:T(8,128)(2,1)S(1)} all-gather(bf16[8,1024]{1,0:T(8,128)(2,1)S(1)} %reduce_sum.22), channel_id=5, replica_groups=mesh['x1'=2,'x0'=2,'y2'=2,'y1'=2,'y0'=2,'z2'=2,'z1'=2,'z0'=2,'core'=2] {..., dimensions={0}, use_global_device_ids=true | all-gather | bytes 49152 | tf_op jit(solution)/shard_map/all_gather | solution.py:165
  114.2 0.6 pad_maximum_fusion.2
  (13 shorter events, 0.2 us)
Async XLA Ops:
  0.6 11.8 %copy-start.3 = (bf16[512,448]{0,1:T(8,128)(2,1)S(1)}, bf16[512,448]{0,1:T(8,128)(2,1)}, u32[]{:S(2)}) copy-start(bf16[512,448]{0,1:T(8,128)(2,1)} %param.7) | copy-start | bytes 1376260
  1.4 13.5 %copy-start.4 = (bf16[512,448]{0,1:T(8,128)(2,1)S(1)}, bf16[512,448]{0,1:T(8,128)(2,1)}, u32[]{:S(2)}) copy-start(bf16[512,448]{0,1:T(8,128)(2,1)} %param.8) | copy-start | bytes 1376260
  2.2 20.7 %all-to-all-start = ((bf16[16,8,1024]{2,1,0:T(8,128)(2,1)}), bf16[16,8,1024]{2,1,0:T(8,128)(2,1)S(1)}, u32[]{:S(2)}, u32[]{:S(2)}) async-start(bf16[16,8,1024]{2,1,0:T(8,128)(2,1)} %bitcast.2), calls=%async_computation | async-start | bytes 524288 | tf_op jit(solution)/shard_map/all_to_all | solution.py:148
  14.9 2.6 %copy-start.5 = (bf16[448,512]{1,0:T(8,128)(2,1)S(1)}, bf16[448,512]{1,0:T(8,128)(2,1)}, u32[]{:S(2)}) copy-start(bf16[448,512]{1,0:T(8,128)(2,1)} %param.9) | copy-start | bytes 1376260
  23.0 16.0 %copy-start.2 = (bf16[896,512]{1,0:T(8,128)(2,1)S(1)}, bf16[896,512]{1,0:T(8,128)(2,1)}, u32[]{:S(2)}) copy-start(bf16[896,512]{1,0:T(8,128)(2,1)} %all-gather.2) | copy-start | bytes 2752516
  84.2 1.5 %copy-start = (bf16[3,8,56,256]{3,2,1,0:T(8,128)(2,1)}, bf16[3,8,56,256]{3,2,1,0:T(8,128)(2,1)S(1)}, u32[]{:S(2)}) copy-start(bf16[3,8,56,256]{3,2,1,0:T(8,128)(2,1)S(1)} %copy.9) | copy-start | bytes 2064388
  85.8 7.6 %copy-start.1 = (bf16[3,8,56,256]{3,2,1,0:T(8,128)(2,1)S(1)}, bf16[3,8,56,256]{3,2,1,0:T(8,128)(2,1)}, u32[]{:S(2)}) copy-start(bf16[3,8,56,256]{3,2,1,0:T(8,128)(2,1)} %copy-done) | copy-start | bytes 2064388
  85.8 22.2 %all-to-all-start.4 = ((bf16[32,8,1024]{2,1,0:T(8,128)(2,1)}), bf16[32,8,1024]{2,1,0:T(8,128)(2,1)S(1)}, u32[]{:S(2)}, u32[]{:S(2)}) async-start(bf16[32,8,1024]{2,1,0:T(8,128)(2,1)} %bitcast.12), calls=%async_computation.4 | async-start | bytes 1048576 | tf_op jit(solution)/shard_map/all_to_all | solution.py:163
  93.3 12.0 %collective-permute-start = (bf16[3,448,256]{2,1,0:T(8,128)(2,1)S(1)}, bf16[3,448,256]{2,1,0:T(8,128)(2,1)S(1)}, u32[]{:S(2)}, u32[]{:S(2)}) collective-permute-start(bf16[3,448,256]{2,1,0:T(8,128)(2,1)S(1)} %bitcast.32), channel_id=1, source_target_pairs={{0,1},{1,0},{2,3},{3,2},{4,5},{5,4},{6,7},{7,6},{8,9},{9,8},{10,11... | collective-permute-start | bytes 2064392 | tf_op jit(solution)/shard_map/ppermute | solution.py:181
